TPU v7x, 256 devices: a whole 4x4x8 slice. The times are simulated.
256 devices in a mesh: dp: 16 (over y, x_lo, core), mp: 16 (over z, x_hi).
Axes of the slice: x: 4 (x_hi: 2, x_lo: 2; x = x_hi * 2 + x_lo), y: 4, z: 8, core: 2. Of those that a mesh axis runs over, the one named last changes fastest.
Arguments:
- hidden: bfloat16 [32768, 7168], P('dp', 'mp'), may hold values from -32 to 32
- cotangent: bfloat16 [32768, 4096], P(('dp', 'mp')), may hold values from -128 to 128
- master: float32 [4096, 7168], P('dp', 'mp'), may hold values from -0.0625 to 0.0625
- moment_one: float32 [4096, 7168], P('dp', 'mp'), may hold values from -0.00048828125 to 0.00048828125
- moment_two: float32 [4096, 7168], P('dp', 'mp'), may hold values from 6.811959e-11 to 6.8119594e-09
Outputs:
- hidden_grad: bfloat16 [32768, 7168], P('dp', 'mp')
- new_weight: bfloat16 [4096, 7168], P(None, 'mp')
- new_master: float32 [4096, 7168], P('dp', 'mp')
- new_moment_one: float32 [4096, 7168], P('dp', 'mp')
- new_moment_two: float32 [4096, 7168], P('dp', 'mp')
All inputs are finite; a program needn't handle non-finite values.
Results may differ from a plain program's by a relative error of at most 0.0049.
Values may be sent and summed in bfloat16 or wider, within the bound.
A program may use at most 128 MiB of HBM per device.

v0:
```python
import jax
import jax.numpy as jnp
from jax import lax
from jax.sharding import PartitionSpec as P


def local(hidden, cotangent, master, moment_one, moment_two):
    own_rows = master.astype(jnp.bfloat16)
    weight = lax.all_gather(own_rows, "dp", axis=0, tiled=True)
    full_cotangent = lax.all_gather(cotangent, "mp", axis=0, tiled=True)
    hidden_grad = jnp.dot(full_cotangent, weight, preferred_element_type=jnp.float32).astype(
        jnp.bfloat16
    )
    gradient = lax.psum_scatter(
        lax.dot_general(
            full_cotangent, hidden, (((0,), (0,)), ((), ())), preferred_element_type=jnp.float32
        ),
        "dp",
        scatter_dimension=0,
        tiled=True,
    )
    squares = lax.psum(jnp.sum(gradient * gradient), ("dp", "mp"))
    scale = jnp.minimum(1.0, 1.0 / (jnp.sqrt(squares) + 1e-06))
    clipped = scale * gradient
    new_moment_one = 0.9 * moment_one + 0.1 * clipped
    new_moment_two = 0.95 * moment_two + 0.05 * clipped * clipped
    first_hat = new_moment_one / (1.0 - 0.9**10)
    second_hat = new_moment_two / (1.0 - 0.95**10)
    new_master = master - 0.01 * (first_hat / (jnp.sqrt(second_hat) + 1e-08) + 0.1 * master)
    new_weight = lax.all_gather(new_master.astype(jnp.bfloat16), "dp", axis=0, tiled=True)
    return (hidden_grad, new_weight, new_master, new_moment_one, new_moment_two)


def solution(mesh):
    return jax.shard_map(
        local,
        mesh=mesh,
        in_specs=(
            P("dp", "mp"),
            P(("dp", "mp"), None),
            P("dp", "mp"),
            P("dp", "mp"),
            P("dp", "mp"),
        ),
        out_specs=(P("dp", "mp"), P(None, "mp"), P("dp", "mp"), P("dp", "mp"), P("dp", "mp")),
        check_vma=False,
    )
```

profile of v0, /device:TPU:1, one launch (start us, length us, event | category | flops | bytes accessed | tf_op | source)
XLA Modules:
  0.0 522.8 jit_solution(17849089691036679413)
XLA Ops:
  7.2 0.0 copy-start
  7.2 0.0 all-gather.4.cloned.1.call-start
  7.2 0.7 all-gather.4.cloned.1.call-update
  7.9 0.0 reduce-scatter.2.cloned.1.call-start
  8.0 231.1 %all-gather.4.cloned.1.call-done = bf16[2048,4096]{1,0:T(8,128)(2,1)} async-done(((bf16[128,4096]{1,0:T(8,128)(2,1)}), bf16[2048,4096]{1,0:T(8,128)(2,1)}) %all-gather.4.cloned.1.call-update) | async-done | bytes 16777232 | tf_op jit(solution)/shard_map/all_gather | solution.py:10
  239.1 0.0 copy-done
  239.1 13.1 %fusion.3 = f32[4096,448]{0,1:T(8,128)} fusion(bf16[2048,448]{0,1:T(8,128)(2,1)S(1)} %copy-done, bf16[2048,4096]{1,0:T(8,128)(2,1)} %all-gather.4.cloned.1.call-done), kind=kOutput, calls=%fused_computation.7 | convolution fusion | flops 7516192768 | bytes 25952256 | tf_op jit(solution)/shard_map/dot_general | solution.py:15
  252.2 0.0 copy-start.1
  252.2 0.0 copy-start.2
  252.2 0.0 copy-start.3
  252.2 0.0 reduce-scatter.2.cloned.1.call-update
  252.2 0.0 all-gather.6.cloned.1.call-start
  252.3 85.5 %reduce-scatter.2.cloned.1.call-done = f32[256,448]{0,1:T(8,128)} async-done(((f32[4096,448]{0,1:T(8,128)}), f32[256,448]{0,1:T(8,128)}) %reduce-scatter.2.cloned.1.call-update) | async-done | bytes 458768 | tf_op jit(solution)/shard_map/reduce_scatter | solution.py:14
  337.8 1.7 multiply_reduce_fusion
  339.5 77.4 %psum.7 = f32[]{:T(128)} all-reduce(f32[]{:T(128)} %multiply_reduce_fusion), channel_id=1, replica_groups=mesh['dp'=16,'mp'=16] {'dp','mp'}, use_global_device_ids=true, to_apply=%region_2.0 | all-reduce | flops 1 | bytes 8 | tf_op jit(solution)/shard_map/psum | solution.py:22
  417.6 0.0 copy-done.1
  417.6 0.0 copy-done.2
  417.6 0.0 copy-done.3
  417.6 2.5 fusion.1
  420.1 0.0 all-gather.6.cloned.1.call-update
  420.1 0.0 all-gather.8.cloned.1.call-start
  420.2 0.5 all-gather.8.cloned.1.call-update
  420.7 43.1 %all-gather.6.cloned.1.call-done = bf16[4096,448]{0,1:T(8,128)(2,1)} async-done(((bf16[256,448]{0,1:T(8,128)(2,1)}), bf16[4096,448]{0,1:T(8,128)(2,1)}) %all-gather.6.cloned.1.call-update) | async-done | bytes 3670032 | tf_op jit(solution)/shard_map/all_gather | solution.py:9
  463.8 13.3 %convolution_convert_fusion = bf16[2048,448]{0,1:T(8,128)(2,1)} fusion(bf16[2048,4096]{1,0:T(8,128)(2,1)} %all-gather.4.cloned.1.call-done, bf16[4096,448]{0,1:T(8,128)(2,1)} %all-gather.6.cloned.1.call-done), kind=kOutput, calls=%fused_computation | convolution fusion | flops 7517110272 | bytes 22282240 | tf_op jit(solution)/shard_map/dot_general | solution.py:11
  477.1 34.9 %all-gather.8.cloned.1.call-done = bf16[4096,448]{0,1:T(8,128)(2,1)} async-done(((bf16[256,448]{0,1:T(8,128)(2,1)}), bf16[4096,448]{0,1:T(8,128)(2,1)}) %all-gather.8.cloned.1.call-update) | async-done | bytes 3670032 | tf_op jit(solution)/shard_map/all_gather | solution.py:30
  512.0 4.3 copy.11
Async XLA Ops:
  7.2 231.9 %copy-start = (bf16[2048,448]{0,1:T(8,128)(2,1)S(1)}, bf16[2048,448]{0,1:T(8,128)(2,1)}, u32[]{:S(2)}) copy-start(bf16[2048,448]{0,1:T(8,128)(2,1)} %param.5) | copy-start | bytes 5505028
  7.2 231.9 %all-gather.4.cloned.1.call-start = ((), (), s32[]{:S(2)}) async-start(), calls=%async_computation.1 | async-start | bytes 17825792 | tf_op jit(solution)/shard_map/all_gather | solution.py:10
  7.9 329.9 %reduce-scatter.2.cloned.1.call-start = ((), (), s32[]{:S(2)}) async-start(), calls=%async_computation.3 | async-start | bytes 7798784 | tf_op jit(solution)/shard_map/reduce_scatter | solution.py:14
  252.2 165.4 %copy-start.1 = (f32[256,448]{0,1:T(8,128)S(1)}, f32[256,448]{0,1:T(8,128)}, u32[]{:S(2)}) copy-start(f32[256,448]{0,1:T(8,128)} %param.7) | copy-start | bytes 1376260
  252.2 165.4 %copy-start.2 = (f32[256,448]{0,1:T(8,128)S(1)}, f32[256,448]{0,1:T(8,128)}, u32[]{:S(2)}) copy-start(f32[256,448]{0,1:T(8,128)} %param.8) | copy-start | bytes 1376260
  252.2 165.4 %copy-start.3 = (f32[256,448]{0,1:T(8,128)S(1)}, f32[256,448]{0,1:T(8,128)}, u32[]{:S(2)}) copy-start(f32[256,448]{0,1:T(8,128)} %param.9) | copy-start | bytes 1376260
  252.2 211.5 %all-gather.6.cloned.1.call-start = ((), (), s32[]{:S(2)}) async-start(), calls=%async_computation.2 | async-start | bytes 3899392 | tf_op jit(solution)/shard_map/all_gather | solution.py:9
  420.1 91.8 %all-gather.8.cloned.1.call-start = ((), (), s32[]{:S(2)}) async-start(), calls=%async_computation.4 | async-start | bytes 3899392 | tf_op jit(solution)/shard_map/all_gather | solution.py:30
Sparse Core Ops, SparseCore 0:
  10.6 228.4 all-gather.3
  252.4 85.3 reduce-scatter.1
  420.2 43.4 all-gather.5
  466.0 45.9 all-gather.7
where the time goes:
time: 523 us
  waiting for transfers between devices  396 us (76%)
  blocking collectives  77.4 us (15%)
  matrix products  26.5 us (5%)
  between operations  14.5 us (3%)
    all_gather x1, waiting for transfers between devices, local(): full_cotangent = lax.all_gather(cotangent, 'mp', axis=0, tiled=True)  231 us
    reduce_scatter x1, waiting for transfers between devices, local(): lax.psum_scatter(lax.dot_general(full_cotangent, hidden, (((0,), (0,)), (...  85.5 us
    psum x1, blocking collectives, local(): squares = lax.psum(jnp.sum(gradient * gradient), ('dp', 'mp'))  77.4 us
    all_gather x1, waiting for transfers between devices, local(): weight = lax.all_gather(own_rows, 'dp', axis=0, tiled=True)  43.1 us
    all_gather x1, waiting for transfers between devices, local(): lax.all_gather(new_master.astype(jnp.bfloat16), 'dp', axis=0, tiled=True)  34.9 us
    dot_general x1, matrix products, local(): jnp.dot(full_cotangent, weight, preferred_element_type=jnp.float32)  13.3 us
    dot_general x1, matrix products, local(): lax.dot_general(full_cotangent, hidden, (((0,), (0,)), ((), ())), preferr...  13.1 us
  transfers between devices with their start and end apart: 4, of which 4 were waited for; matrix products, arithmetic and copies ran while one was open for 3% of the time, Pallas kernels for 0%

commit v1 on v0

v1 whole, which is shorter than its diff:
```python
import functools

import jax
import jax.numpy as jnp
from jax import lax
from jax.experimental import pallas as pl
from jax.experimental.pallas import tpu as pltpu
from jax.sharding import PartitionSpec as P

F32 = jnp.float32
BF16 = jnp.bfloat16
NT = (((1,), (1,)), ((), ()))
MESH = pl.DeviceIdType.MESH
FC = 448
NK = 8


def rem(a, n):
    return lax.rem(a, jnp.int32(n))


def div(a, n):
    return lax.div(a, jnp.int32(n))


def kernel(
    hid, cot, mas, m1, m2,
    hg_out, nw_out, nm_out, n1_out, n2_out,
    cbuf, wbuf, hbuf, ht, hts, hrel, gs, gr,
    yfs, yfr, yns, ynr, xs, xr, ga, acc, hgs, hgrel,
    masb, m1b, m2b, nwv, ns, nr,
    lsem, csem, zs, zr, hss, hsr, wxs, wxr, wys, wyr, wds, wdr,
    ds_, dr, yf_s, yf_r, yn_s, yn_r, x_s, x_r, g_s, g_r, n_s, n_r, o_s, o_r,
):
    dp = lax.axis_index("dp")
    mp = lax.axis_index("mp")
    core = rem(dp, 2)
    xlo = rem(div(dp, 2), 2)
    y = div(dp, 4)
    h = rem(mp, 2)
    z = div(mp, 2)
    x = h * 2 + xlo
    xr1, xl1, x2 = rem(x + 1, 4), rem(x + 3, 4), rem(x + 2, 4)
    yr1, yl1, y2 = rem(y + 1, 4), rem(y + 3, 4), rem(y + 2, 4)

    def dev(xx=x, yy=y, zz=z, cc=core):
        return ((yy * 2 + rem(xx, 2)) * 2 + cc, zz * 2 + div(xx, 2))

    def rc(src, dst, ss, rs, to):
        return pltpu.make_async_remote_copy(
            src_ref=src, dst_ref=dst, send_sem=ss, recv_sem=rs, device_id=to, device_id_type=MESH
        )

    me = dev(cc=1 - core)
    sib = dev(cc=1 - core)

    loads = [
        pltpu.make_async_copy(mas, masb, lsem.at[0]),
        pltpu.make_async_copy(hid, hbuf, lsem.at[1]),
        pltpu.make_async_copy(m1, m1b, lsem.at[2]),
        pltpu.make_async_copy(m2, m2b, lsem.at[3]),
    ]
    zrow = pl.multiple_of(z * 128, 128)
    for k in range(NK):
        q, p = k // 2, 1 - k % 2
        r, half = q // 2, q % 2
        xl_ = 1 - xlo if r else xlo
        c_ = 1 - core if p else core
        for yy in range(4):
            off = pl.multiple_of(((yy * 2 + xl_) * 2 + c_) * 256 + half * 128, 128)
            pltpu.make_async_copy(
                cot.at[:, pl.ds(off, 128)],
                cbuf.at[k, pl.ds(zrow, 128), pl.ds(yy * 128, 128)],
                csem.at[k],
            ).start()
        if k == 0:
            loads[0].start()
            loads[1].start()
    loads[2].start()
    loads[3].start()

    barrier = pltpu.get_barrier_semaphore()
    peers = [sib]
    for xx in (xr1, xl1, x2):
        peers += [dev(xx=xx), dev(xx=xx, cc=1 - core)]
    peers += [dev(yy=yy) for yy in (yr1, yl1, y2)]
    peers += [dev(zz=rem(z + i, 8)) for i in range(1, 8)]
    for to in peers:
        pl.semaphore_signal(barrier, inc=1, device_id=to, device_id_type=MESH)
    pl.semaphore_wait(barrier, len(peers))

    zto = (dev(zz=rem(z + 1, 8)), dev(zz=rem(z + 7, 8)))

    def zcopy(d, k, hop, sending):
        if d == 0:
            slot = rem(z + 16 - hop - (0 if sending else 1), 8)
        else:
            slot = rem(z + hop + (0 if sending else 1), 8)
        row, n = slot * 128, 128
        if hop == 3:
            n = 64
            row = row + 64 * d
        ref = cbuf.at[k, pl.ds(pl.multiple_of(row, 64), n), :]
        return rc(ref, ref, zs.at[d, k, hop], zr.at[d, k, hop], zto[d])

    def zring(s):
        for hop in (3, 2, 1, 0):
            k = s - hop

            @pl.when((k >= 0) & (k < NK))
            def _(hop=hop, k=k):
                if hop == 0:
                    own = cbuf.at[k, pl.ds(zrow, 128), :]
                    pltpu.make_async_copy(own, own, csem.at[k]).wait()
                for d in (0, 1):
                    if hop > 0:
                        zcopy(d, k, hop - 1, False).wait_recv()
                    zcopy(d, k, hop, True).start()

    eye = (
        lax.broadcasted_iota(jnp.int32, (FC, FC), 0) == lax.broadcasted_iota(jnp.int32, (FC, FC), 1)
    ).astype(BF16)

    def wblk(xx, yy, p, rows=None):
        lanes = pl.ds(pl.multiple_of(yy * 128, 128), 128)
        r_ = slice(None) if rows is None else pl.ds(rows[0], rows[1])
        return wbuf.at[rem(xx, 2), :, p, div(xx, 2), r_, lanes]

    def wx(d, far, sending):
        to = dev(xx=xr1 if d == 0 else xl1)
        if not far:
            src = x if sending else (xl1 if d == 0 else xr1)
            blk = wblk(src, y, 0)
        else:
            src = (xl1 if d == 0 else xr1) if sending else x2
            blk = wblk(src, y, 0, (d * 224, 224))
        i = 2 * far + d
        return rc(blk, blk, wxs.at[i], wxr.at[i], to)

    def wy(j, d, far, sending):
        xx = rem(x + j, 4)
        to = dev(yy=yr1 if d == 0 else yl1)
        if not far:
            src = y if sending else (yl1 if d == 0 else yr1)
            blk = wblk(xx, src, 0)
        else:
            src = (yl1 if d == 0 else yr1) if sending else y2
            blk = wblk(xx, src, 0, (d * 224, 224))
        i = 2 * far + d
        return rc(blk, blk, wys.at[j, i], wyr.at[j, i], to)

    def wd(j):
        xx = rem(x + j, 4)
        src = wbuf.at[rem(xx, 2), :, 0, div(xx, 2), :, :]
        dst = wbuf.at[rem(xx, 2), :, 1, div(xx, 2), :, :]
        return rc(src, dst, wds.at[j], wdr.at[j], sib)

    def hsend(d):
        src = hts.at[pl.ds(d * 224, 224), :]
        return rc(src, hrel.at[d], hss.at[d], hsr.at[d], dev(xx=xr1 if d == 0 else xl1))

    def hforward(d):
        to = dev(xx=xr1 if d == 0 else xl1)
        f_src = div(xl1 if d == 0 else xr1, 2)
        dst = ht.at[f_src, pl.ds(d * 224, 224), :]
        return rc(hrel.at[d], dst, hss.at[2 + d], hsr.at[2 + d], to)

    def hwait(d):
        dst = ht.at[1 - h, pl.ds(d * 224, 224), :]
        rc(dst, dst, hss.at[2 + d], hsr.at[2 + d], sib).wait_recv()

    def gd(q, f):
        return rc(gs.at[q, f], gr.at[q, f], ds_.at[q, f], dr.at[q, f], sib)

    def gyfar(q, f):
        return rc(
            yfs.at[q, f], yfr.at[q, f], yf_s.at[q, f], yf_r.at[q, f], dev(yy=yr1 if f == 0 else yl1)
        )

    def gynear(q, d):
        return rc(
            yns.at[q, d], ynr.at[q, d], yn_s.at[q, d], yn_r.at[q, d], dev(yy=yr1 if d == 0 else yl1)
        )

    def lanes(yy):
        return pl.ds(pl.multiple_of(yy * 128, 128), 128)

    def gradient_chunk(kc):
        q = div(kc, 2)
        part = kc - 2 * q
        for d in (0, 1):
            zcopy(d, kc, 3, False).wait_recv()

        @pl.when(part == 0)
        def _():
            def body(f, c):
                gs[q, f] = jnp.dot(ht[f], cbuf[kc], preferred_element_type=F32)
                gd(q, f).start()
                return c

            lax.fori_loop(0, 2, body, 0)

        @pl.when(part == 1)
        def _():
            def body(f, c):
                gd(q, f).wait_recv()
                gr[q, f] = gr[q, f] + jnp.dot(ht[f], cbuf[kc], preferred_element_type=F32)
                yfs[q, f] = gr[q, f, :, lanes(y2)].astype(BF16)
                return c

            lax.fori_loop(0, 2, body, 0)
            for f in (0, 1):
                gyfar(q, f).start()

    def ystep2(q):
        for f in (0, 1):
            gyfar(q, f).wait_recv()
        yns[q, 0, 0] = (gr[q, 0, :, lanes(yr1)] + yfr[q, 0].astype(F32)).astype(BF16)
        yns[q, 0, 1] = gr[q, 1, :, lanes(yr1)].astype(BF16)
        gynear(q, 0).start()
        yns[q, 1, 0] = gr[q, 0, :, lanes(yl1)].astype(BF16)
        yns[q, 1, 1] = (gr[q, 1, :, lanes(yl1)] + yfr[q, 1].astype(F32)).astype(BF16)
        gynear(q, 1).start()

    def xsend(q, i, sending):
        half = q % 2
        if q < 2:
            return rc(xs.at[q, 0], xr.at[half, 2], x_s.at[q, 0], x_r.at[half, 2], dev(xx=x2))
        if sending:
            return rc(
                xs.at[q, i], xr.at[half, h], x_s.at[q, i], x_r.at[half, h], dev(xx=i * 2 + 1 - xlo)
            )
        return rc(xs.at[q, i], xr.at[half, i], x_s.at[q, i], x_r.at[half, i], dev(xx=x2))

    def ystep3(q):
        for d in (0, 1):
            gynear(q, d).wait_recv()

        def total(f):
            return (
                gr[q, f, :, lanes(y)] + ynr[q, 0, f].astype(F32) + ynr[q, 1, f].astype(F32)
            )

        if q < 2:
            ga[q] = total(h)
            xs[q, 0] = total(1 - h).astype(BF16)
            xsend(q, 0, True).start()
        else:
            for f in (0, 1):
                xs[q, f] = total(f).astype(BF16)
                xsend(q, f, True).start()

    def wchunk(u, p, f):
        r, half = div(u, 2), rem(u, 2)
        xl_ = xlo + r - 2 * xlo * r
        return wbuf[xl_, half, p, f]

    def hg_pair(u):
        def body(i, c):
            f, t = div(i, 4), rem(i, 4)
            rows = pl.ds(pl.multiple_of(t * 256, 256), 256)
            a = lax.dot_general(cbuf[2 * u, rows, :], wchunk(u, 1, f), NT, preferred_element_type=F32)
            a += lax.dot_general(
                cbuf[2 * u + 1, rows, :], wchunk(u, 0, f), NT, preferred_element_type=F32
            )

            @pl.when(u == 0)
            def _():
                acc[f, rows, :] = a

            @pl.when((u > 0) & (u < 3))
            def _():
                acc[f, rows, :] = acc[f, rows, :] + a

            @pl.when(u == 3)
            def _():
                out = (acc[f, rows, :] + a).astype(BF16)
                hgs[f, pl.ds(2 * t, 2)] = out.reshape(2, 128, FC)

            return c

        lax.fori_loop(0, 8, body, 0)

    def hgsend(d):
        src = hgs.at[1 - h, pl.ds(4 * d, 4)]
        return rc(src, hgrel.at[d], g_s.at[d], g_r.at[d], dev(xx=xr1 if d == 0 else xl1))

    def hgforward(d):
        to = dev(xx=xr1 if d == 0 else xl1)
        par = div(xl1 if d == 0 else xr1, 2)
        return rc(hgrel.at[d], hg_out.at[pl.ds(4 * d, 4), par], g_s.at[2 + d], g_r.at[2 + d], to)

    def hgwait(d):
        dst = hg_out.at[pl.ds(4 * d, 4), 1 - h]
        rc(dst, dst, g_s.at[2 + d], g_r.at[2 + d], sib).wait_recv()

    zring(jnp.int32(0))
    loads[0].wait()
    wt = lax.dot_general(eye, masb[...].astype(BF16), NT, preferred_element_type=F32).astype(BF16)
    for half in (0, 1):
        wbuf[xlo, half, 0, h, :, lanes(y)] = wt[:, half * 128 : half * 128 + 128]
    wx(0, 0, True).start()
    wx(1, 0, True).start()
    wy(0, 0, 0, True).start()
    wy(0, 1, 0, True).start()
    loads[1].wait()

    def transpose_hidden(par, dst):
        for t in range(4):
            b = hbuf[pl.ds(2 * t, 2), par].reshape(256, FC)
            dst[:, t * 256 : t * 256 + 256] = lax.dot_general(
                eye, b, NT, preferred_element_type=F32
            ).astype(BF16)

    transpose_hidden(1 - h, hts)
    for d in (0, 1):
        hsend(d).start()
    transpose_hidden(h, ht.at[h])

    def tick(s, c):
        zring(s)

        @pl.when(s == 1)
        def _():
            for d in (0, 1):
                wx(d, 0, False).wait_recv()
            for d in (0, 1):
                wx(d, 1, True).start()
            for j in (1, 3):
                for d in (0, 1):
                    wy(j, d, 0, True).start()

        @pl.when(s == 2)
        def _():
            for d in (0, 1):
                wx(d, 1, False).wait_recv()
            for d in (0, 1):
                wy(2, d, 0, True).start()

        @pl.when(s == 3)
        def _():
            for d in (0, 1):
                hsend(d).wait_recv()
                hforward(d).start()

        @pl.when(s == 4)
        def _():
            for d in (0, 1):
                hwait(d)

        @pl.when(s == 5)
        def _():
            for j in range(4):
                for d in (0, 1):
                    wy(j, d, 0, False).wait_recv()
                    wy(j, d, 1, True).start()

        @pl.when(s == 7)
        def _():
            for j in range(4):
                for d in (0, 1):
                    wy(j, d, 1, False).wait_recv()
                wd(j).start()

        for q in range(3):

            @pl.when(s == 6 + 2 * q)
            def _(q=q):
                ystep2(q)

            @pl.when(s == 7 + 2 * q)
            def _(q=q):
                ystep3(q)

        @pl.when(s >= 4)
        def _():
            gradient_chunk(s - 4)

        @pl.when(s == 8)
        def _():
            for j in range(4):
                wd(j).wait_recv()

        @pl.when(s >= 8)
        def _():
            hg_pair(s - 8)

        return c

    lax.fori_loop(1, 12, tick, 0)

    for d in (0, 1):
        hgsend(d).start()
    own_hg = pltpu.make_async_copy(hgs.at[h], hg_out.at[:, h], lsem.at[4])
    own_hg.start()
    ystep2(3)
    ystep3(3)
    for d in (0, 1):
        hgsend(d).wait_recv()
        hgforward(d).start()
    loads[2].wait()
    loads[3].wait()
    sq = jnp.zeros((8, 128), F32)
    gt = []
    for half in (0, 1):
        xsend(half, 0, False).wait_recv()
        for i in (0, 1):
            xsend(2 + half, i, False).wait_recv()
        g = (
            ga[half]
            + xr[half, 2].astype(F32)
            + xr[half, 0].astype(F32)
            + xr[half, 1].astype(F32)
        )
        ga[half] = g
        sq = sq + jnp.sum((g * g).reshape(FC // 8, 8, 128), axis=0)

    groups = [
        [dev(cc=1 - core)]
        + [dev(xx=rem(x + i, 4), cc=c_) for i in (1, 2, 3) for c_ in (core, 1 - core)],
        [dev(yy=rem(y + i, 4)) for i in (1, 2, 3)],
        [dev(zz=rem(z + i, 8)) for i in range(1, 8)],
    ]
    sends = []
    for ph, group in enumerate(groups):
        ns[ph] = sq
        cps = [
            rc(ns.at[ph], nr.at[ph, i], n_s.at[ph, i], n_r.at[ph, i], to)
            for i, to in enumerate(group)
        ]
        for cp in cps:
            cp.start()
        sends += cps
        for i, cp in enumerate(cps):
            cp.wait_recv()
            sq = sq + nr[ph, i]
    squares = jnp.sum(sq, keepdims=True)
    scale = jnp.minimum(1.0, 1.0 / (jnp.sqrt(squares) + 1e-06))

    for half in (0, 1):
        rows = pl.ds(half * 128, 128)
        clipped = scale * jnp.transpose(ga[half])
        nm1 = 0.9 * m1b[rows, :] + 0.1 * clipped
        nm2 = 0.95 * m2b[rows, :] + 0.05 * clipped * clipped
        first_hat = nm1 / (1.0 - 0.9**10)
        second_hat = nm2 / (1.0 - 0.95**10)
        w = masb[rows, :]
        nmas = w - 0.01 * (first_hat / (jnp.sqrt(second_hat) + 1e-08) + 0.1 * w)
        m1b[rows, :] = nm1
        m2b[rows, :] = nm2
        masb[rows, :] = nmas
        nwv[rows, :] = nmas.astype(BF16)

    def nblk(yy, j, half=None, cc=core):
        xl_ = 1 - xlo if j else xlo
        off = ((yy * 2 + xl_) * 2 + cc) * 256
        if half is None:
            return nw_out.at[pl.ds(pl.multiple_of(off, 256), 256), :]
        return nw_out.at[pl.ds(pl.multiple_of(off + half * 128, 128), 128), :]

    def cp(src, dst, i, to):
        return rc(src, dst, o_s.at[i], o_r.at[i], to)

    to_y = (dev(yy=yr1), dev(yy=yl1))
    from_y = (yl1, yr1)
    to_x = dev(xx=h * 2 + 1 - xlo)
    outs = []

    def go(c):
        c.start()
        outs.append(c)

    def await_(blk, i):
        cp(blk, blk, i, sib).wait_recv()

    go(cp(nwv, nblk(y, 0), 8, to_x))
    for d in (0, 1):
        go(cp(nwv, nblk(y, 0), d, to_y[d]))
    go(cp(nwv, nblk(y, 0), 9, sib))
    finals = [
        pltpu.make_async_copy(nwv, nblk(y, 0), lsem.at[0]),
        pltpu.make_async_copy(masb, nm_out, lsem.at[1]),
        pltpu.make_async_copy(m1b, n1_out, lsem.at[2]),
        pltpu.make_async_copy(m2b, n2_out, lsem.at[3]),
    ]
    for c in finals:
        c.start()
    b = nblk(y, 1)
    await_(b, 8)
    for d in (0, 1):
        go(cp(b, b, 2 + d, to_y[d]))
    go(cp(b, b, 10, sib))
    for j in (0, 1):
        for d in (0, 1):
            b = nblk(from_y[d], j)
            await_(b, 2 * j + d)
            half = nblk(from_y[d], j, d)
            go(cp(half, half, 4 + 2 * j + d, to_y[d]))
            go(cp(b, b, 11 + 2 * j + d, sib))
    for j in (0, 1):
        for d in (0, 1):
            await_(nblk(y2, j, d), 4 + 2 * j + d)
        b = nblk(y2, j)
        go(cp(b, b, 15 + j, sib))
    oc = 1 - core
    await_(nblk(y, 0, cc=oc), 9)
    await_(nblk(y, 1, cc=oc), 10)
    for j in (0, 1):
        for d in (0, 1):
            await_(nblk(from_y[d], j, cc=oc), 11 + 2 * j + d)
        await_(nblk(y2, j, cc=oc), 15 + j)

    for d in (0, 1):
        hgwait(d)
    own_hg.wait()
    for c in finals:
        c.wait()
    for c in outs + sends:
        c.wait_send()
    for d in (0, 1):
        hgsend(d).wait_send()
        hgforward(d).wait_send()
        hsend(d).wait_send()
        hforward(d).wait_send()
        for far in (0, 1):
            wx(d, far, True).wait_send()
            for j in range(4):
                wy(j, d, far, True).wait_send()
    for j in range(4):
        wd(j).wait_send()
    for q in range(4):
        for f in (0, 1):
            gd(q, f).wait_send()
            gyfar(q, f).wait_send()
            gynear(q, f).wait_send()
            if q >= 2 or f == 0:
                xsend(q, f, True).wait_send()

    def drain(k, c):
        for hop in range(4):
            for d in (0, 1):
                zcopy(d, k, hop, True).wait_send()
        return c

    lax.fori_loop(0, NK, drain, 0)


def local(hidden, cotangent, master, moment_one, moment_two):
    dma = pltpu.SemaphoreType.DMA
    any_ = pl.BlockSpec(memory_space=pl.ANY)
    v = pltpu.VMEM
    scratch = [
        v((NK, 1024, 512), BF16),
        v((2, 2, 2, 2, FC, 512), BF16),
        v((8, 2, 128, FC), BF16),
        v((2, FC, 1024), BF16),
        v((FC, 1024), BF16),
        v((2, 224, 1024), BF16),
        v((4, 2, FC, 512), F32),
        v((4, 2, FC, 512), F32),
        v((4, 2, FC, 128), BF16),
        v((4, 2, FC, 128), BF16),
        v((4, 2, 2, FC, 128), BF16),
        v((4, 2, 2, FC, 128), BF16),
        v((4, 2, FC, 128), BF16),
        v((2, 3, FC, 128), BF16),
        v((2, FC, 128), F32),
        v((2, 1024, FC), F32),
        v((2, 8, 128, FC), BF16),
        v((2, 4, 128, FC), BF16),
        v((256, FC), F32),
        v((256, FC), F32),
        v((256, FC), F32),
        v((256, FC), BF16),
        v((3, 8, 128), F32),
        v((3, 7, 8, 128), F32),
        dma((5,)),
        dma((NK,)),
        dma((2, NK, 4)), dma((2, NK, 4)),
        dma((4,)), dma((4,)),
        dma((4,)), dma((4,)),
        dma((4, 4)), dma((4, 4)),
        dma((4,)), dma((4,)),
        dma((4, 2)), dma((4, 2)),
        dma((4, 2)), dma((4, 2)),
        dma((4, 2)), dma((4, 2)),
        dma((4, 2)), dma((2, 3)),
        dma((4,)), dma((4,)),
        dma((3, 7)), dma((3, 7)),
        dma((17,)), dma((17,)),
    ]
    sds = jax.ShapeDtypeStruct
    hg, nw, nm, n1, n2 = pl.pallas_call(
        kernel,
        out_shape=(
            sds((8, 2, 128, FC), BF16),
            sds((4096, FC), BF16),
            sds((256, FC), F32),
            sds((256, FC), F32),
            sds((256, FC), F32),
        ),
        in_specs=[any_] * 5,
        out_specs=(any_,) * 5,
        scratch_shapes=scratch,
        compiler_params=pltpu.CompilerParams(
            collective_id=0, has_side_effects=True, vmem_limit_bytes=63 * 2**20
        ),
        cost_estimate=pl.CostEstimate(
            flops=15_032_385_536, bytes_accessed=16_000_000, transcendentals=0
        ),
        name="fused_backward",
    )(hidden.reshape(8, 2, 128, FC), cotangent, master, moment_one, moment_two)
    return (hg.reshape(2048, FC), nw, nm, n1, n2)


def solution(mesh):
    return jax.shard_map(
        local,
        mesh=mesh,
        in_specs=(
            P("dp", "mp"),
            P(("dp", "mp"), None),
            P("dp", "mp"),
            P("dp", "mp"),
            P("dp", "mp"),
        ),
        out_specs=(P("dp", "mp"), P(None, "mp"), P("dp", "mp"), P("dp", "mp"), P("dp", "mp")),
        check_vma=False,
    )
```

time: 523 us -> 186 us (0.36)
  waiting for transfers between devices: 396 us -> 0 us
  Pallas kernels: 0 us -> 164 us
  blocking collectives: 77.4 us -> 0 us
  matrix products: 26.5 us -> 0 us
  local copies, waits for them, and re-layouts: 4.32 us -> 20.7 us
  between operations: 14.5 us -> 0.69 us
    all_gather x3 -> x0, waiting for transfers between devices: 309 us -> none  [the longest x1 231 us: local(): full_cotangent = lax.all_gather(cotangent, 'mp', axis=0, tiled=True)]
    pallas_call x0 -> x1, Pallas kernels: none -> 164 us  [local(): pl.pallas_call(kernel, out_shape=(sds((8, 2, 128, FC), BF16), sds((4096,...]
    reduce_scatter x1 -> x0, waiting for transfers between devices: 85.5 us -> none  [local(): lax.psum_scatter(lax.dot_general(full_cotangent, hidden, (((0,), (0,)), (...]
    psum x1 -> x0, blocking collectives: 77.4 us -> none  [local(): squares = lax.psum(jnp.sum(gradient * gradient), ('dp', 'mp'))]
    dot_general x2 -> x0, matrix products: 26.5 us -> none  [the longest x1 13.3 us: local(): jnp.dot(full_cotangent, weight, preferred_element_type=jnp.float32)]
    unnamed x9 -> x19, local copies, waits for them, and re-layouts: 4.32 us -> 20.7 us
  transfers between devices with their start and end apart: 4 -> 0, of which waited for: 4 -> 0; matrix products, arithmetic and copies ran while one was open for 3% -> 0% of each run, Pallas kernels for 0% -> 0%
where the time goes in v1:
time: 186 us
  Pallas kernels  164 us (88%)
  local copies, waits for them, and re-layouts  20.7 us (11%)
    pallas_call x1, Pallas kernels, local(): pl.pallas_call(kernel, out_shape=(sds((8, 2, 128, FC), BF16), sds((4096,...  164 us
    unnamed x19, local copies, waits for them, and re-layouts  20.7 us

profile of v1, /device:TPU:1, one launch (start us, length us, event | category | flops | bytes accessed | tf_op | source)
XLA Modules:
  0.0 185.8 jit_solution(59396621903649148)
XLA Ops:
  0.6 0.0 copy-start.4
  0.6 0.0 copy-start
  0.7 2.2 %copy.11.mas = f32[256,448]{1,0:T(8,128)} copy(f32[256,448]{0,1:T(8,128)} %param.7) | data formatting | bytes 917504 | tf_op args[2]
  2.8 2.0 %copy.12.m1 = f32[256,448]{1,0:T(8,128)} copy(f32[256,448]{0,1:T(8,128)} %param.8) | data formatting | bytes 917504 | tf_op args[3]
  4.8 0.0 copy-done.4
  4.8 1.0 copy.13.m2
  5.8 0.0 copy-done
  5.8 2.4 %copy.10 = bf16[2048,448]{1,0:T(8,128)(2,1)} copy(bf16[2048,448]{0,1:T(8,128)(2,1)S(1)} %copy-done) | data formatting | bytes 3670016 | tf_op args[0]
  8.3 164.4 %fused_backward.1 = (bf16[8,2,128,448]{3,2,1,0:T(8,128)(2,1)}, bf16[4096,448]{1,0:T(8,128)(2,1)}, f32[256,448]{1,0:T(8,128)}, f32[256,448]{1,0:T(8,128)}, f32[256,448]{1,0:T(8,128)}) custom-call(bf16[8,2,128,448]{3,2,1,0:T(8,128)(2,1)} %bitcast.3, bf16[128,4096]{1,0:T(8,128)(2,1)} %cot.1, f32[256,448]{1,0:T(8,128)} %copy.11.mas, f32[256,448]{1,0:T(8,128)} %copy.12.m1, ...), custom_call_target="tpu_custom_call" | custom-call | flops 15032385536 | bytes 16000000 | tf_op jit(solution)/shard_map/fused_backward/pallas_call | solution.py:593
  172.7 0.0 copy-start.3
  172.7 0.0 copy-start.2
  172.7 0.0 copy-start.1
  172.7 4.0 %copy.14 = bf16[2048,448]{0,1:T(8,128)(2,1)} copy(bf16[2048,448]{1,0:T(8,128)(2,1)} %bitcast.2) | data formatting | bytes 3670016
  176.7 0.0 copy-done.3
  176.7 1.0 copy.16
  177.6 0.0 copy-done.2
  177.6 1.0 copy.17
  178.6 0.0 copy-done.1
  178.6 1.0 copy.18
  179.5 6.3 %copy.15 = bf16[4096,448]{0,1:T(8,128)(2,1)} copy(bf16[4096,448]{1,0:T(8,128)(2,1)} %get-tuple-element.16) | data formatting | bytes 7340032
Async XLA Ops:
  0.6 4.2 %copy-start.4 = (f32[256,448]{0,1:T(8,128)S(1)}, f32[256,448]{0,1:T(8,128)}, u32[]{:S(2)}) copy-start(f32[256,448]{0,1:T(8,128)} %param.9) | copy-start | bytes 1376260
  0.6 5.2 %copy-start = (bf16[2048,448]{0,1:T(8,128)(2,1)S(1)}, bf16[2048,448]{0,1:T(8,128)(2,1)}, u32[]{:S(2)}) copy-start(bf16[2048,448]{0,1:T(8,128)(2,1)} %param.5) | copy-start | bytes 5505028
  172.7 4.0 %copy-start.3 = (f32[256,448]{1,0:T(8,128)S(1)}, f32[256,448]{1,0:T(8,128)}, u32[]{:S(2)}) copy-start(f32[256,448]{1,0:T(8,128)} %get-tuple-element.17) | copy-start | bytes 1376260
  172.7 4.9 %copy-start.2 = (f32[256,448]{1,0:T(8,128)S(1)}, f32[256,448]{1,0:T(8,128)}, u32[]{:S(2)}) copy-start(f32[256,448]{1,0:T(8,128)} %get-tuple-element.18) | copy-start | bytes 1376260
  172.7 5.9 %copy-start.1 = (f32[256,448]{1,0:T(8,128)S(1)}, f32[256,448]{1,0:T(8,128)}, u32[]{:S(2)}) copy-start(f32[256,448]{1,0:T(8,128)} %get-tuple-element.19) | copy-start | bytes 1376260

commit v2 on v1

v2 whole, which is shorter than its diff:
```python
import functools

import jax
import jax.numpy as jnp
from jax import lax
from jax.experimental import pallas as pl
from jax.experimental.pallas import tpu as pltpu
from jax.sharding import PartitionSpec as P

F32 = jnp.float32
BF16 = jnp.bfloat16
NT = (((1,), (1,)), ((), ()))
MESH = pl.DeviceIdType.MESH
FC = 448
NK = 8


def rem(a, n):
    return lax.rem(a, jnp.int32(n))


def div(a, n):
    return lax.div(a, jnp.int32(n))


def kernel(
    hid, cot, mas, m1, m2,
    hg_out, nw_out, nm_out, n1_out, n2_out,
    cbuf, wbuf, ht, hts, gs, gr,
    yfs, yfr, yns, ynr, xs, xr, ga, acc, hgs,
    masb, m1b, m2b, nwb, ns, nr,
    lsem, csem, zs, zr, hss, hsr, wxs, wxr, wys, wyr, wds, wdr,
    ds_, dr, yf_s, yf_r, yn_s, yn_r, x_s, x_r, g_s, g_r, n_s, n_r, o_s, o_r, w_s,
):
    dp = lax.axis_index("dp")
    mp = lax.axis_index("mp")
    core = rem(dp, 2)
    xlo = rem(div(dp, 2), 2)
    y = div(dp, 4)
    h = rem(mp, 2)
    z = div(mp, 2)
    x = h * 2 + xlo
    xr1, xl1, x2 = rem(x + 1, 4), rem(x + 3, 4), rem(x + 2, 4)
    yr1, yl1, y2 = rem(y + 1, 4), rem(y + 3, 4), rem(y + 2, 4)

    def dev(xx=x, yy=y, zz=z, cc=core):
        return ((yy * 2 + rem(xx, 2)) * 2 + cc, zz * 2 + div(xx, 2))

    def rc(src, dst, ss, rs, to):
        return pltpu.make_async_remote_copy(
            src_ref=src, dst_ref=dst, send_sem=ss, recv_sem=rs, device_id=to, device_id_type=MESH
        )

    sib = dev(cc=1 - core)

    loads = [
        pltpu.make_async_copy(mas, masb, lsem.at[0]),
        pltpu.make_async_copy(m1, m1b, lsem.at[1]),
        pltpu.make_async_copy(m2, m2b, lsem.at[2]),
    ]
    zrow = pl.multiple_of(z * 128, 128)
    for k in range(NK):
        q, p = k // 2, 1 - k % 2
        r, half = q // 2, q % 2
        xl_ = 1 - xlo if r else xlo
        c_ = 1 - core if p else core
        for yy in range(4):
            off = pl.multiple_of(((yy * 2 + xl_) * 2 + c_) * 256 + half * 128, 128)
            pltpu.make_async_copy(
                cot.at[:, pl.ds(off, 128)],
                cbuf.at[k, pl.ds(zrow, 128), pl.ds(yy * 128, 128)],
                csem.at[k],
            ).start()
        if k == 0:
            loads[0].start()
            for par, sem in ((1 - h, 3), (h, 4)):
                for t in range(8):
                    src = hid.at[:, pl.ds(pl.multiple_of((2 * t + par) * 128, 128), 128)]
                    dst = hts if sem == 3 else ht.at[h]
                    dst = dst.at[:, pl.ds(t * 128, 128)]
                    pltpu.make_async_copy(src, dst, lsem.at[sem]).start()
    loads[1].start()
    loads[2].start()

    barrier = pltpu.get_barrier_semaphore()
    peers = [sib]
    for xx in (xr1, xl1, x2):
        peers += [dev(xx=xx), dev(xx=xx, cc=1 - core)]
    peers += [dev(yy=yy) for yy in (yr1, yl1, y2)]
    peers += [dev(zz=rem(z + i, 8)) for i in range(1, 8)]
    for to in peers:
        pl.semaphore_signal(barrier, inc=1, device_id=to, device_id_type=MESH)
    pl.semaphore_wait(barrier, len(peers))

    zto = (dev(zz=rem(z + 1, 8)), dev(zz=rem(z + 7, 8)))

    def zcopy(d, k, hop, sending):
        if d == 0:
            slot = rem(z + 16 - hop - (0 if sending else 1), 8)
        else:
            slot = rem(z + hop + (0 if sending else 1), 8)
        row, n = slot * 128, 128
        if hop == 3:
            n = 64
            row = row + 64 * d
        ref = cbuf.at[k, pl.ds(pl.multiple_of(row, 64), n), :]
        return rc(ref, ref, zs.at[d, k, hop], zr.at[d, k, hop], zto[d])

    def zown(k):
        own = cbuf.at[k, pl.ds(zrow, 128), :]
        pltpu.make_async_copy(own, own, csem.at[k]).wait()
        for d in (0, 1):
            zcopy(d, k, 0, True).start()

    def zring(s):
        for hop in (3, 2, 1):
            k = s - hop

            @pl.when((k >= 0) & (k < NK))
            def _(hop=hop, k=k):
                for d in (0, 1):
                    zcopy(d, k, hop - 1, False).wait_recv()
                    zcopy(d, k, hop, True).start()

        @pl.when(s < NK - 1)
        def _():
            zown(s + 1)

    def wblk(xx, yy, p, rows=None):
        lanes = pl.ds(pl.multiple_of(yy * 128, 128), 128)
        r_ = slice(None) if rows is None else pl.ds(rows[0], rows[1])
        return wbuf.at[rem(xx, 2), :, p, div(xx, 2), r_, lanes]

    def wx(d, far, sending):
        to = dev(xx=xr1 if d == 0 else xl1)
        if not far:
            src = x if sending else (xl1 if d == 0 else xr1)
            blk = wblk(src, y, 0)
        else:
            src = (xl1 if d == 0 else xr1) if sending else x2
            blk = wblk(src, y, 0, (d * 224, 224))
        i = 2 * far + d
        return rc(blk, blk, wxs.at[i], wxr.at[i], to)

    def wy(j, d, far, sending):
        xx = rem(x + j, 4)
        to = dev(yy=yr1 if d == 0 else yl1)
        if not far:
            src = y if sending else (yl1 if d == 0 else yr1)
            blk = wblk(xx, src, 0)
        else:
            src = (yl1 if d == 0 else yr1) if sending else y2
            blk = wblk(xx, src, 0, (d * 224, 224))
        i = 2 * far + d
        return rc(blk, blk, wys.at[j, i], wyr.at[j, i], to)

    def wd(j):
        xx = rem(x + j, 4)
        src = wbuf.at[rem(xx, 2), :, 0, div(xx, 2), :, :]
        dst = wbuf.at[rem(xx, 2), :, 1, div(xx, 2), :, :]
        return rc(src, dst, wds.at[j], wdr.at[j], sib)

    def hsend(d, sending):
        rows = pl.ds(d * 224, 224)
        dst = ht.at[h if sending else 1 - h, rows, :]
        return rc(hts.at[rows, :], dst, hss.at[d], hsr.at[d], dev(xx=x2))

    def gd(q, f):
        return rc(gs.at[q, f], gr.at[q, f], ds_.at[q, f], dr.at[q, f], sib)

    def gyfar(q, f):
        return rc(
            yfs.at[q, f], yfr.at[q, f], yf_s.at[q, f], yf_r.at[q, f], dev(yy=yr1 if f == 0 else yl1)
        )

    def gynear(q, d):
        return rc(
            yns.at[q, d], ynr.at[q, d], yn_s.at[q, d], yn_r.at[q, d], dev(yy=yr1 if d == 0 else yl1)
        )

    def lanes(yy):
        return pl.ds(pl.multiple_of(yy * 128, 128), 128)

    def gradient_chunk(kc):
        q = div(kc, 2)
        part = kc - 2 * q
        for d in (0, 1):
            zcopy(d, kc, 3, False).wait_recv()

        @pl.when(part == 0)
        def _():
            def body(f, c):
                gs[q, f] = jnp.dot(ht[f], cbuf[kc], preferred_element_type=F32)
                gd(q, f).start()
                return c

            lax.fori_loop(0, 2, body, 0)

        @pl.when(part == 1)
        def _():
            for f in (0, 1):
                gd(q, f).wait_recv()
                gr[q, f] = gr[q, f] + jnp.dot(ht[f], cbuf[kc], preferred_element_type=F32)
                yfs[q, f] = gr[q, f, :, lanes(y2)].astype(BF16)
                gyfar(q, f).start()

    def ystep2(q):
        gyfar(q, 0).wait_recv()
        yns[q, 0, 0] = (gr[q, 0, :, lanes(yr1)] + yfr[q, 0].astype(F32)).astype(BF16)
        yns[q, 0, 1] = gr[q, 1, :, lanes(yr1)].astype(BF16)
        gynear(q, 0).start()
        gyfar(q, 1).wait_recv()
        yns[q, 1, 0] = gr[q, 0, :, lanes(yl1)].astype(BF16)
        yns[q, 1, 1] = (gr[q, 1, :, lanes(yl1)] + yfr[q, 1].astype(F32)).astype(BF16)
        gynear(q, 1).start()

    def xsend(q, i, sending):
        half = q % 2
        if q < 2:
            return rc(xs.at[q, 0], xr.at[half, 2], x_s.at[q, 0], x_r.at[half, 2], dev(xx=x2))
        if sending:
            return rc(
                xs.at[q, i], xr.at[half, h], x_s.at[q, i], x_r.at[half, h], dev(xx=i * 2 + 1 - xlo)
            )
        return rc(xs.at[q, i], xr.at[half, i], x_s.at[q, i], x_r.at[half, i], dev(xx=x2))

    def ystep3(q):
        for d in (0, 1):
            gynear(q, d).wait_recv()

        def total(f):
            return (
                gr[q, f, :, lanes(y)] + ynr[q, 0, f].astype(F32) + ynr[q, 1, f].astype(F32)
            )

        if q < 2:
            ga[q] = total(h)
            xs[q, 0] = total(1 - h).astype(BF16)
            xsend(q, 0, True).start()
        else:
            for f in (0, 1):
                xs[q, f] = total(f).astype(BF16)
                xsend(q, f, True).start()

    def hg_tile(k, f, toks):
        u = div(k, 2)
        r, half, p = div(u, 2), rem(u, 2), 1 - rem(k, 2)
        w = wbuf[xlo + r - 2 * xlo * r, half, p, f]
        return lax.dot_general(w, cbuf[k, toks, :], NT, preferred_element_type=F32)

    def tile(i):
        return div(i, 4), pl.ds(pl.multiple_of(rem(i, 4) * 256, 256), 256)

    def hg_first():
        def body(i, c):
            f, toks = tile(i)
            acc[f, :, toks] = hg_tile(0, f, toks) + hg_tile(1, f, toks)
            return c

        lax.fori_loop(0, 8, body, 0)

    def hg_add(k):
        k = jnp.int32(k)

        def body(i, c):
            f, toks = tile(i)
            acc[f, :, toks] = acc[f, :, toks] + hg_tile(k, f, toks) + hg_tile(k + 1, f, toks)
            return c

        lax.fori_loop(0, 8, body, 0)

    def hg_one(k):
        def body(i, c):
            f, toks = tile(i)
            acc[f, :, toks] = acc[f, :, toks] + hg_tile(k, f, toks)
            return c

        lax.fori_loop(0, 8, body, 0)

    def hg_last(f):
        def body(i, c):
            toks = tile(i)[1]
            a = hg_tile(jnp.int32(5), f, toks) + hg_tile(jnp.int32(6), f, toks)
            a += hg_tile(jnp.int32(7), f, toks)
            hgs[f, :, toks] = (acc[f, :, toks] + a).astype(BF16)
            return c

        lax.fori_loop(0, 4, body, 0)

    def hgout(t, par):
        return hg_out.at[:, pl.ds(pl.multiple_of((2 * t + par) * 128, 128), 128)]

    def hgsend(t, sending):
        src = hgs.at[1 - h, :, pl.ds(t * 128, 128)]
        dst = hgout(t, h if sending else 1 - h)
        return rc(src, dst, g_s.at[t], g_r.at[t], dev(xx=x2))

    def own_hg_copy():
        for t in range(8):
            src = hgs.at[h, :, pl.ds(t * 128, 128)]
            pltpu.make_async_copy(src, hgout(t, h), lsem.at[4]).start()

    zown(jnp.int32(0))
    zown(jnp.int32(1))
    loads[0].wait()
    for half in (0, 1):
        wbuf[xlo, half, 0, h, :, lanes(y)] = masb[:, half * 128 : half * 128 + 128].astype(BF16)
    wx(0, 0, True).start()
    wx(1, 0, True).start()
    wy(0, 0, 0, True).start()
    wy(0, 1, 0, True).start()
    pltpu.make_async_copy(hts, ht.at[h], lsem.at[4]).wait()

    def tick(s, c):
        zring(s)

        @pl.when(s == 2)
        def _():
            for d in (0, 1):
                wx(d, 0, False).wait_recv()
            for d in (0, 1):
                wx(d, 1, True).start()
            for j in (1, 3):
                for d in (0, 1):
                    wy(j, d, 0, True).start()
            pltpu.make_async_copy(hts, hts, lsem.at[3]).wait()
            for d in (0, 1):
                hsend(d, True).start()

        @pl.when(s == 3)
        def _():
            for d in (0, 1):
                wx(d, 1, False).wait_recv()
            for d in (0, 1):
                wy(2, d, 0, True).start()

        @pl.when(s == 4)
        def _():
            for j in range(4):
                for d in (0, 1):
                    wy(j, d, 0, False).wait_recv()
                    wy(j, d, 1, True).start()

        @pl.when(s == 5)
        def _():
            for d in (0, 1):
                hsend(d, False).wait_recv()
            gradient_chunk(jnp.int32(0))
            for j in range(4):
                for d in (0, 1):
                    wy(j, d, 1, False).wait_recv()
                wd(j).start()

        @pl.when(s == 6)
        def _():
            gradient_chunk(jnp.int32(1))

        @pl.when(s >= 6)
        def _():
            gradient_chunk(s - 4)

        for q in range(3):

            @pl.when(s == (7, 8, 10)[q])
            def _(q=q):
                ystep2(q)

        for q in range(2):

            @pl.when(s == (8, 9)[q])
            def _(q=q):
                ystep3(q)

        @pl.when(s == 6)
        def _():
            for j in range(4):
                wd(j).wait_recv()
            hg_first()

        @pl.when(s == 7)
        def _():
            hg_add(2)

        @pl.when(s == 8)
        def _():
            hg_one(jnp.int32(4))

        return c

    lax.fori_loop(1, 12, tick, 0)

    hg_last(1 - h)
    ystep2(3)
    for t in range(2):
        hgsend(t, True).start()
    ystep3(2)
    hg_last(h)
    own_hg_copy()
    ystep3(3)
    loads[1].wait()
    loads[2].wait()
    sq = jnp.zeros((8, 128), F32)
    gt = []
    for half in (0, 1):
        xsend(half, 0, False).wait_recv()
        for i in (0, 1):
            xsend(2 + half, i, False).wait_recv()
        g = (
            ga[half]
            + xr[half, 2].astype(F32)
            + xr[half, 0].astype(F32)
            + xr[half, 1].astype(F32)
        )
        ga[half] = g
        sq = sq + jnp.sum((g * g).reshape(FC // 8, 8, 128), axis=0)

    groups = [
        [dev(cc=1 - core)]
        + [dev(xx=rem(x + i, 4), cc=c_) for i in (1, 2, 3) for c_ in (core, 1 - core)],
        [dev(yy=rem(y + i, 4)) for i in (1, 2, 3)],
        [dev(zz=rem(z + i, 8)) for i in range(1, 8)],
    ]
    sends = []
    for ph, group in enumerate(groups):
        ns[ph] = sq
        cps = [
            rc(ns.at[ph], nr.at[ph, i], n_s.at[ph, i], n_r.at[ph, i], to)
            for i, to in enumerate(group)
        ]
        for cp in cps:
            cp.start()
        sends += cps
        for i, cp in enumerate(cps):
            cp.wait_recv()
            sq = sq + nr[ph, i]
        if ph == 0:
            for t in range(2, 5):
                hgsend(t, True).start()
    squares = jnp.sum(sq, keepdims=True)
    scale = jnp.minimum(1.0, 1.0 / (jnp.sqrt(squares) + 1e-06))

    for half in (0, 1):
        cols = pl.ds(half * 128, 128)
        clipped = scale * ga[half]
        nm1 = 0.9 * m1b[:, cols] + 0.1 * clipped
        nm2 = 0.95 * m2b[:, cols] + 0.05 * clipped * clipped
        first_hat = nm1 / (1.0 - 0.9**10)
        second_hat = nm2 / (1.0 - 0.95**10)
        w = masb[:, cols]
        nmas = w - 0.01 * (first_hat / (jnp.sqrt(second_hat) + 1e-08) + 0.1 * w)
        m1b[:, cols] = nm1
        m2b[:, cols] = nm2
        masb[:, cols] = nmas
        nwb[:, pl.ds(pl.multiple_of(dp * 256 + half * 128, 128), 128)] = nmas.astype(BF16)

    def nblk(yy, j, half=None, cc=core):
        xl_ = 1 - xlo if j else xlo
        off = ((yy * 2 + xl_) * 2 + cc) * 256
        rows = slice(None) if half is None else pl.ds(half * 224, 224)
        return nwb.at[rows, pl.ds(pl.multiple_of(off, 256), 256)]

    def cp(src, dst, i, to):
        return rc(src, dst, o_s.at[i], o_r.at[i], to)

    to_y = (dev(yy=yr1), dev(yy=yl1))
    from_y = (yl1, yr1)
    to_x = dev(xx=h * 2 + 1 - xlo)
    outs, puts = [], []

    def go(c):
        c.start()
        outs.append(c)

    def put(yy, j, cc=core):
        off = pl.multiple_of(((yy * 2 + (1 - xlo if j else xlo)) * 2 + cc) * 256, 256)
        c = pltpu.make_async_copy(
            nblk(yy, j, cc=cc), nw_out.at[:, pl.ds(off, 256)], w_s.at[len(puts)]
        )
        c.start()
        puts.append(c)

    def await_(blk, i):
        cp(blk, blk, i, sib).wait_recv()

    go(cp(nblk(y, 0), nblk(y, 0), 8, to_x))
    for d in (0, 1):
        go(cp(nblk(y, 0), nblk(y, 0), d, to_y[d]))
    go(cp(nblk(y, 0), nblk(y, 0), 9, sib))
    put(y, 0)
    finals = [
        pltpu.make_async_copy(masb, nm_out, lsem.at[1]),
        pltpu.make_async_copy(m1b, n1_out, lsem.at[2]),
        pltpu.make_async_copy(m2b, n2_out, lsem.at[3]),
    ]
    for c in finals:
        c.start()
    for d in (0, 1):
        b = nblk(from_y[d], 0)
        await_(b, d)
        part = nblk(from_y[d], 0, d)
        go(cp(part, part, 4 + d, to_y[d]))
        go(cp(b, b, 11 + d, sib))
        put(from_y[d], 0)
    b = nblk(y, 1)
    await_(b, 8)
    for d in (0, 1):
        go(cp(b, b, 2 + d, to_y[d]))
    go(cp(b, b, 10, sib))
    put(y, 1)
    for t in range(5, 8):
        hgsend(t, True).start()
    b = nblk(y2, 0)
    for d in (0, 1):
        await_(nblk(y2, 0, d), 4 + d)
    go(cp(b, b, 6, to_x))
    go(cp(b, b, 15, sib))
    put(y2, 0)
    for d in (0, 1):
        b = nblk(from_y[d], 1)
        await_(b, 2 + d)
        go(cp(b, b, 13 + d, sib))
        put(from_y[d], 1)
    b = nblk(y2, 1)
    await_(b, 6)
    go(cp(b, b, 16, sib))
    put(y2, 1)
    oc = 1 - core
    for i, (yy, j) in enumerate(
        ((y, 0), (y, 1), (yl1, 0), (yr1, 0), (yl1, 1), (yr1, 1), (y2, 0), (y2, 1))
    ):
        await_(nblk(yy, j, cc=oc), 9 + i)
        put(yy, j, oc)

    for t in range(8):
        hgsend(t, False).wait_recv()
    pltpu.make_async_copy(hts, hts, lsem.at[4]).wait()
    for c in finals + puts:
        c.wait()
    for c in outs + sends:
        c.wait_send()
    for d in (0, 1):
        hsend(d, True).wait_send()
        for far in (0, 1):
            wx(d, far, True).wait_send()
            for j in range(4):
                wy(j, d, far, True).wait_send()
    for j in range(4):
        wd(j).wait_send()
    for t in range(8):
        hgsend(t, True).wait_send()
    for q in range(4):
        for f in (0, 1):
            gd(q, f).wait_send()
            gyfar(q, f).wait_send()
            gynear(q, f).wait_send()
            if q >= 2 or f == 0:
                xsend(q, f, True).wait_send()

    def drain(k, c):
        for hop in range(4):
            for d in (0, 1):
                zcopy(d, k, hop, True).wait_send()
        return c

    lax.fori_loop(0, NK, drain, 0)


def local(hidden, cotangent, master, moment_one, moment_two):
    dma = pltpu.SemaphoreType.DMA
    any_ = pl.BlockSpec(memory_space=pl.ANY)
    v = pltpu.VMEM
    scratch = [
        v((NK, 1024, 512), BF16),
        v((2, 2, 2, 2, FC, 512), BF16),
        v((2, FC, 1024), BF16),
        v((FC, 1024), BF16),
        v((4, 2, FC, 512), F32),
        v((4, 2, FC, 512), F32),
        v((4, 2, FC, 128), BF16),
        v((4, 2, FC, 128), BF16),
        v((4, 2, 2, FC, 128), BF16),
        v((4, 2, 2, FC, 128), BF16),
        v((4, 2, FC, 128), BF16),
        v((2, 3, FC, 128), BF16),
        v((2, FC, 128), F32),
        v((2, FC, 1024), F32),
        v((2, FC, 1024), BF16),
        v((FC, 256), F32),
        v((FC, 256), F32),
        v((FC, 256), F32),
        v((FC, 4096), BF16),
        v((3, 8, 128), F32),
        v((3, 7, 8, 128), F32),
        dma((5,)),
        dma((NK,)),
        dma((2, NK, 4)), dma((2, NK, 4)),
        dma((2,)), dma((2,)),
        dma((4,)), dma((4,)),
        dma((4, 4)), dma((4, 4)),
        dma((4,)), dma((4,)),
        dma((4, 2)), dma((4, 2)),
        dma((4, 2)), dma((4, 2)),
        dma((4, 2)), dma((4, 2)),
        dma((4, 2)), dma((2, 3)),
        dma((8,)), dma((8,)),
        dma((3, 7)), dma((3, 7)),
        dma((17,)), dma((17,)),
        dma((16,)),
    ]
    sds = jax.ShapeDtypeStruct
    hg, nw, nm, n1, n2 = pl.pallas_call(
        kernel,
        out_shape=(
            sds((FC, 2048), BF16),
            sds((FC, 4096), BF16),
            sds((FC, 256), F32),
            sds((FC, 256), F32),
            sds((FC, 256), F32),
        ),
        in_specs=[any_] * 5,
        out_specs=(any_,) * 5,
        scratch_shapes=scratch,
        compiler_params=pltpu.CompilerParams(
            collective_id=0, has_side_effects=True, vmem_limit_bytes=63 * 2**20
        ),
        cost_estimate=pl.CostEstimate(
            flops=15_032_385_536, bytes_accessed=16_000_000, transcendentals=0
        ),
        name="fused_backward",
    )(hidden.T, cotangent, master.T, moment_one.T, moment_two.T)
    outs = (hg, nw, nm, n1, n2)
    hg, nw, nm, n1, n2 = pl.pallas_call(
        hand_on,
        out_shape=tuple(sds(t.shape, t.dtype) for t in outs),
        in_specs=[any_] * 5,
        out_specs=(any_,) * 5,
        scratch_shapes=[v(t.shape, t.dtype) for t in outs] + [dma((2, 11))],
        compiler_params=pltpu.CompilerParams(vmem_limit_bytes=60 * 2**20),
        name="hand_on",
    )(*outs)
    return (hg.T, nw.T, nm.T, n1.T, n2.T)


def hand_on(*refs):
    srcs, dsts, bufs, sems = refs[:5], refs[5:10], refs[10:15], refs[15]
    ins, outs = [], []
    for src, dst, buf in zip(srcs, dsts, bufs):
        n = 4 if src.shape[1] > 256 else 1
        rows = FC // n
        for i in range(n):
            cut = pl.ds(i * rows, rows)
            k = len(ins)
            ins.append(pltpu.make_async_copy(src.at[cut, :], buf.at[cut, :], sems.at[0, k]))
            outs.append(pltpu.make_async_copy(buf.at[cut, :], dst.at[cut, :], sems.at[1, k]))
    for c in ins:
        c.start()
    for c, d in zip(ins, outs):
        c.wait()
        d.start()
    for d in outs:
        d.wait()


def solution(mesh):
    return jax.shard_map(
        local,
        mesh=mesh,
        in_specs=(
            P("dp", "mp"),
            P(("dp", "mp"), None),
            P("dp", "mp"),
            P("dp", "mp"),
            P("dp", "mp"),
        ),
        out_specs=(P("dp", "mp"), P(None, "mp"), P("dp", "mp"), P("dp", "mp"), P("dp", "mp")),
        check_vma=False,
    )
```

time: 186 us -> 156 us (0.84)
  local copies, waits for them, and re-layouts: 20.7 us -> 0 us
  Pallas kernels: 164 us -> 155 us
    unnamed x19 -> x0, local copies, waits for them, and re-layouts: 20.7 us -> none
    pallas_call x1 -> x2, Pallas kernels: 164 us -> 155 us  [the longest x1 149 us: local(): pl.pallas_call(kernel, out_shape=(sds((FC, 2048), BF16), sds((FC, 4096),...]
where the time goes in v2:
time: 156 us
  Pallas kernels  155 us (99%)
    pallas_call x1, Pallas kernels, local(): pl.pallas_call(kernel, out_shape=(sds((FC, 2048), BF16), sds((FC, 4096),...  149 us
    pallas_call x1, Pallas kernels, local(): pl.pallas_call(hand_on, out_shape=tuple((sds(t.shape, t.dtype) for t in o...  5.56 us

profile of v2, /device:TPU:1, one launch (start us, length us, event | category | flops | bytes accessed | tf_op | source)
XLA Modules:
  0.0 155.6 jit_solution(18277989998913227513)
XLA Ops:
  0.6 149.4 %fused_backward.1 = (bf16[448,2048]{1,0:T(8,128)(2,1)}, bf16[448,4096]{1,0:T(8,128)(2,1)}, f32[448,256]{1,0:T(8,128)}, f32[448,256]{1,0:T(8,128)}, f32[448,256]{1,0:T(8,128)}) custom-call(bf16[448,2048]{1,0:T(8,128)(2,1)} %bitcast.10, bf16[128,4096]{1,0:T(8,128)(2,1)} %cot.1, f32[448,256]{1,0:T(8,128)} %bitcast.12, f32[448,256]{1,0:T(8,128)} %bitcast.13, ...), custom_call_target="tpu_custom_call" | custom-call | flops 15032385536 | bytes 16000000 | tf_op jit(solution)/shard_map/fused_backward/pallas_call | solution.py:611
  150.0 5.6 %hand_on.1 = (bf16[448,2048]{1,0:T(8,128)(2,1)}, bf16[448,4096]{1,0:T(8,128)(2,1)}, f32[448,256]{1,0:T(8,128)}, f32[448,256]{1,0:T(8,128)}, f32[448,256]{1,0:T(8,128)}) custom-call(bf16[448,2048]{1,0:T(8,128)(2,1)} %get-tuple-element.15.refs_0_, bf16[448,4096]{1,0:T(8,128)(2,1)} %get-tuple-element.16.refs_1_, f32[448,256]{1,0:T(8,128)} %get-tuple-element.17.refs_2_, ...), custom_call_target="tpu_custom_call" | custom-call | tf_op jit(solution)/shard_map/hand_on/pallas_call | solution.py:632

commit v3 on v2

--- a/solution.py
+++ b/solution.py
@@ -84,9 +84,11 @@
 
     barrier = pltpu.get_barrier_semaphore()
     peers = [sib]
-    for xx in (xr1, xl1, x2):
-        peers += [dev(xx=xx), dev(xx=xx, cc=1 - core)]
-    peers += [dev(yy=yy) for yy in (yr1, yl1, y2)]
+    plane = [
+        dev(xx=rem(x + i, 4), yy=rem(y + j, 4), cc=1 - core if c else core)
+        for j in range(4) for i in range(4) for c in (0, 1) if i + j + c
+    ]
+    peers = list(plane)
     peers += [dev(zz=rem(z + i, 8)) for i in range(1, 8)]
     for to in peers:
         pl.semaphore_signal(barrier, inc=1, device_id=to, device_id_type=MESH)
@@ -94,23 +96,26 @@
 
     zto = (dev(zz=rem(z + 1, 8)), dev(zz=rem(z + 7, 8)))
 
-    def zcopy(d, k, hop, sending):
-        if d == 0:
-            slot = rem(z + 16 - hop - (0 if sending else 1), 8)
-        else:
-            slot = rem(z + hop + (0 if sending else 1), 8)
+    def zcopy(d, k, hop):
+        slot = rem(z + 16 - hop, 8) if d == 0 else rem(z + hop, 8)
         row, n = slot * 128, 128
         if hop == 3:
             n = 64
             row = row + 64 * d
         ref = cbuf.at[k, pl.ds(pl.multiple_of(row, 64), n), :]
-        return rc(ref, ref, zs.at[d, k, hop], zr.at[d, k, hop], zto[d])
+        return rc(ref, ref, zs, zr.at[k, hop], zto[d])
 
     def zown(k):
         own = cbuf.at[k, pl.ds(zrow, 128), :]
         pltpu.make_async_copy(own, own, csem.at[k]).wait()
         for d in (0, 1):
-            zcopy(d, k, 0, True).start()
+            zcopy(d, k, 0).start()
+
+    def got(ref, sem):
+        pltpu.make_async_copy(ref, ref, sem).wait()
+
+    def zwait(k, hop):
+        got(cbuf.at[k, pl.ds(0, 256 if hop < 3 else 128), :], zr.at[k, hop])
 
     def zring(s):
         for hop in (3, 2, 1):
@@ -118,9 +123,9 @@
 
             @pl.when((k >= 0) & (k < NK))
             def _(hop=hop, k=k):
+                zwait(k, hop - 1)
                 for d in (0, 1):
-                    zcopy(d, k, hop - 1, False).wait_recv()
-                    zcopy(d, k, hop, True).start()
+                    zcopy(d, k, hop).start()
 
         @pl.when(s < NK - 1)
         def _():
@@ -131,51 +136,39 @@
         r_ = slice(None) if rows is None else pl.ds(rows[0], rows[1])
         return wbuf.at[rem(xx, 2), :, p, div(xx, 2), r_, lanes]
 
-    def wx(d, far, sending):
-        to = dev(xx=xr1 if d == 0 else xl1)
-        if not far:
-            src = x if sending else (xl1 if d == 0 else xr1)
-            blk = wblk(src, y, 0)
-        else:
-            src = (xl1 if d == 0 else xr1) if sending else x2
-            blk = wblk(src, y, 0, (d * 224, 224))
-        i = 2 * far + d
-        return rc(blk, blk, wxs.at[i], wxr.at[i], to)
-
-    def wy(j, d, far, sending):
-        xx = rem(x + j, 4)
-        to = dev(yy=yr1 if d == 0 else yl1)
-        if not far:
-            src = y if sending else (yl1 if d == 0 else yr1)
-            blk = wblk(xx, src, 0)
-        else:
-            src = (yl1 if d == 0 else yr1) if sending else y2
-            blk = wblk(xx, src, 0, (d * 224, 224))
-        i = 2 * far + d
-        return rc(blk, blk, wys.at[j, i], wyr.at[j, i], to)
+    def wx(d, far):
+        src = x if not far else (xl1 if d == 0 else xr1)
+        blk = wblk(src, y, 0, (d * 224, 224) if far else None)
+        return rc(blk, blk, wxs, wxr.at[far], dev(xx=xr1 if d == 0 else xl1))
+
+    def wy(j, d, far):
+        src = y if not far else (yl1 if d == 0 else yr1)
+        blk = wblk(rem(x + j, 4), src, 0, (d * 224, 224) if far else None)
+        return rc(blk, blk, wys, wyr.at[far], dev(yy=yr1 if d == 0 else yl1))
 
     def wd(j):
         xx = rem(x + j, 4)
         src = wbuf.at[rem(xx, 2), :, 0, div(xx, 2), :, :]
         dst = wbuf.at[rem(xx, 2), :, 1, div(xx, 2), :, :]
-        return rc(src, dst, wds.at[j], wdr.at[j], sib)
-
-    def hsend(d, sending):
+        return rc(src, dst, wds, wdr, sib)
+
+    def hsend(d):
         rows = pl.ds(d * 224, 224)
-        dst = ht.at[h if sending else 1 - h, rows, :]
-        return rc(hts.at[rows, :], dst, hss.at[d], hsr.at[d], dev(xx=x2))
+        dst = ht.at[h, rows, :]
+        return rc(hts.at[rows, :], dst, hss, hsr, dev(xx=x2))
 
     def gd(q, f):
-        return rc(gs.at[q, f], gr.at[q, f], ds_.at[q, f], dr.at[q, f], sib)
+        return rc(gs.at[q, f], gr.at[q, f], ds_, dr.at[q, f], sib)
 
     def gyfar(q, f):
         return rc(
-            yfs.at[q, f], yfr.at[q, f], yf_s.at[q, f], yf_r.at[q, f], dev(yy=yr1 if f == 0 else yl1)
+            yfs.at[q, f], yfr.at[q, f], yf_s, yf_r.at[q, f], dev(yy=yr1 if f == 0 else yl1)
         )
 
-    def gynear(q, d):
+    def gynear(q, d, f):
         return rc(
-            yns.at[q, d], ynr.at[q, d], yn_s.at[q, d], yn_r.at[q, d], dev(yy=yr1 if d == 0 else yl1)
+            yns.at[q, d, f], ynr.at[q, d, f], yn_s, yn_r.at[q],
+            dev(yy=yr1 if d == 0 else yl1),
         )
 
     def lanes(yy):
@@ -184,8 +177,7 @@
     def gradient_chunk(kc):
         q = div(kc, 2)
         part = kc - 2 * q
-        for d in (0, 1):
-            zcopy(d, kc, 3, False).wait_recv()
+        zwait(kc, 3)
 
         @pl.when(part == 0)
         def _():
@@ -203,30 +195,25 @@
                 gr[q, f] = gr[q, f] + jnp.dot(ht[f], cbuf[kc], preferred_element_type=F32)
                 yfs[q, f] = gr[q, f, :, lanes(y2)].astype(BF16)
                 gyfar(q, f).start()
+            for f in (1, 0):
+                yns[q, 1 - f, f] = gr[q, f, :, lanes(yl1 if f == 0 else yr1)].astype(BF16)
+                gynear(q, 1 - f, f).start()
 
     def ystep2(q):
-        gyfar(q, 0).wait_recv()
-        yns[q, 0, 0] = (gr[q, 0, :, lanes(yr1)] + yfr[q, 0].astype(F32)).astype(BF16)
-        yns[q, 0, 1] = gr[q, 1, :, lanes(yr1)].astype(BF16)
-        gynear(q, 0).start()
-        gyfar(q, 1).wait_recv()
-        yns[q, 1, 0] = gr[q, 0, :, lanes(yl1)].astype(BF16)
-        yns[q, 1, 1] = (gr[q, 1, :, lanes(yl1)] + yfr[q, 1].astype(F32)).astype(BF16)
-        gynear(q, 1).start()
-
-    def xsend(q, i, sending):
+        for f in (0, 1):
+            gyfar(q, f).wait_recv()
+            own = gr[q, f, :, lanes(yr1 if f == 0 else yl1)]
+            yns[q, f, f] = (own + yfr[q, f].astype(F32)).astype(BF16)
+            gynear(q, f, f).start()
+
+    def xsend(q, i):
         half = q % 2
         if q < 2:
-            return rc(xs.at[q, 0], xr.at[half, 2], x_s.at[q, 0], x_r.at[half, 2], dev(xx=x2))
-        if sending:
-            return rc(
-                xs.at[q, i], xr.at[half, h], x_s.at[q, i], x_r.at[half, h], dev(xx=i * 2 + 1 - xlo)
-            )
-        return rc(xs.at[q, i], xr.at[half, i], x_s.at[q, i], x_r.at[half, i], dev(xx=x2))
+            return rc(xs.at[q, 0], xr.at[half, 2], x_s, x_r, dev(xx=x2))
+        return rc(xs.at[q, i], xr.at[half, h], x_s, x_r, dev(xx=i * 2 + 1 - xlo))
 
     def ystep3(q):
-        for d in (0, 1):
-            gynear(q, d).wait_recv()
+        got(ynr.at[q], yn_r.at[q])
 
         def total(f):
             return (
@@ -236,11 +223,11 @@
         if q < 2:
             ga[q] = total(h)
             xs[q, 0] = total(1 - h).astype(BF16)
-            xsend(q, 0, True).start()
+            xsend(q, 0).start()
         else:
             for f in (0, 1):
                 xs[q, f] = total(f).astype(BF16)
-                xsend(q, f, True).start()
+                xsend(q, f).start()
 
     def hg_tile(k, f, toks):
         u = div(k, 2)
@@ -290,10 +277,10 @@
     def hgout(t, par):
         return hg_out.at[:, pl.ds(pl.multiple_of((2 * t + par) * 128, 128), 128)]
 
-    def hgsend(t, sending):
+    def hgsend(t):
         src = hgs.at[1 - h, :, pl.ds(t * 128, 128)]
-        dst = hgout(t, h if sending else 1 - h)
-        return rc(src, dst, g_s.at[t], g_r.at[t], dev(xx=x2))
+        dst = hgout(t, h)
+        return rc(src, dst, g_s, g_r, dev(xx=x2))
 
     def own_hg_copy():
         for t in range(8):
@@ -305,50 +292,46 @@
     loads[0].wait()
     for half in (0, 1):
         wbuf[xlo, half, 0, h, :, lanes(y)] = masb[:, half * 128 : half * 128 + 128].astype(BF16)
-    wx(0, 0, True).start()
-    wx(1, 0, True).start()
-    wy(0, 0, 0, True).start()
-    wy(0, 1, 0, True).start()
+    wx(0, 0).start()
+    wx(1, 0).start()
+    wy(0, 0, 0).start()
+    wy(0, 1, 0).start()
     pltpu.make_async_copy(hts, ht.at[h], lsem.at[4]).wait()
 
     def tick(s, c):
         zring(s)
 
-        @pl.when(s == 2)
-        def _():
+        @pl.when(s == 1)
+        def _():
+            got(gs.at[0, 0, pl.ds(0, 224), :], wxr.at[0])
             for d in (0, 1):
-                wx(d, 0, False).wait_recv()
-            for d in (0, 1):
-                wx(d, 1, True).start()
+                wx(d, 1).start()
             for j in (1, 3):
                 for d in (0, 1):
-                    wy(j, d, 0, True).start()
+                    wy(j, d, 0).start()
+
+        @pl.when(s == 2)
+        def _():
+            got(gs.at[0, 0, pl.ds(0, 112), :], wxr.at[1])
+            for d in (0, 1):
+                wy(2, d, 0).start()
             pltpu.make_async_copy(hts, hts, lsem.at[3]).wait()
             for d in (0, 1):
-                hsend(d, True).start()
-
-        @pl.when(s == 3)
-        def _():
-            for d in (0, 1):
-                wx(d, 1, False).wait_recv()
-            for d in (0, 1):
-                wy(2, d, 0, True).start()
+                hsend(d).start()
 
         @pl.when(s == 4)
         def _():
+            got(gs.at[0], wyr.at[0])
             for j in range(4):
                 for d in (0, 1):
-                    wy(j, d, 0, False).wait_recv()
-                    wy(j, d, 1, True).start()
+                    wy(j, d, 1).start()
 
         @pl.when(s == 5)
         def _():
-            for d in (0, 1):
-                hsend(d, False).wait_recv()
+            got(hts, hsr)
             gradient_chunk(jnp.int32(0))
+            got(gs.at[0, 0], wyr.at[1])
             for j in range(4):
-                for d in (0, 1):
-                    wy(j, d, 1, False).wait_recv()
                 wd(j).start()
 
         @pl.when(s == 6)
@@ -373,8 +356,7 @@
 
         @pl.when(s == 6)
         def _():
-            for j in range(4):
-                wd(j).wait_recv()
+            got(gs.at[:, 0], wdr)
             hg_first()
 
         @pl.when(s == 7)
@@ -390,9 +372,9 @@
     lax.fori_loop(1, 12, tick, 0)
 
     hg_last(1 - h)
+    for t in range(2):
+        hgsend(t).start()
     ystep2(3)
-    for t in range(2):
-        hgsend(t, True).start()
     ystep3(2)
     hg_last(h)
     own_hg_copy()
@@ -400,11 +382,8 @@
     loads[1].wait()
     loads[2].wait()
     sq = jnp.zeros((8, 128), F32)
-    gt = []
+    got(xr, x_r)
     for half in (0, 1):
-        xsend(half, 0, False).wait_recv()
-        for i in (0, 1):
-            xsend(2 + half, i, False).wait_recv()
         g = (
             ga[half]
             + xr[half, 2].astype(F32)
@@ -414,28 +393,19 @@
         ga[half] = g
         sq = sq + jnp.sum((g * g).reshape(FC // 8, 8, 128), axis=0)
 
-    groups = [
-        [dev(cc=1 - core)]
-        + [dev(xx=rem(x + i, 4), cc=c_) for i in (1, 2, 3) for c_ in (core, 1 - core)],
-        [dev(yy=rem(y + i, 4)) for i in (1, 2, 3)],
-        [dev(zz=rem(z + i, 8)) for i in range(1, 8)],
-    ]
-    sends = []
+    groups = [plane, [dev(zz=rem(z + i, 8)) for i in range(1, 8)]]
+    base = 0
     for ph, group in enumerate(groups):
         ns[ph] = sq
-        cps = [
-            rc(ns.at[ph], nr.at[ph, i], n_s.at[ph, i], n_r.at[ph, i], to)
-            for i, to in enumerate(group)
-        ]
-        for cp in cps:
-            cp.start()
-        sends += cps
-        for i, cp in enumerate(cps):
-            cp.wait_recv()
-            sq = sq + nr[ph, i]
-        if ph == 0:
+        for i, to in enumerate(group):
+            rc(ns.at[ph], nr.at[base + i], n_s, n_r.at[ph], to).start()
+        if ph == 1:
             for t in range(2, 5):
-                hgsend(t, True).start()
+                hgsend(t).start()
+        heard = nr.at[pl.ds(base, len(group))]
+        got(heard, n_r.at[ph])
+        sq = sq + jnp.sum(heard[...], axis=0)
+        base += len(group)
     squares = jnp.sum(sq, keepdims=True)
     scale = jnp.minimum(1.0, 1.0 / (jnp.sqrt(squares) + 1e-06))
 
@@ -460,24 +430,21 @@
         return nwb.at[rows, pl.ds(pl.multiple_of(off, 256), 256)]
 
     def cp(src, dst, i, to):
-        return rc(src, dst, o_s.at[i], o_r.at[i], to)
+        return rc(src, dst, o_s, o_r.at[i], to)
 
     to_y = (dev(yy=yr1), dev(yy=yl1))
     from_y = (yl1, yr1)
     to_x = dev(xx=h * 2 + 1 - xlo)
-    outs, puts = [], []
 
     def go(c):
         c.start()
-        outs.append(c)
 
     def put(yy, j, cc=core):
         off = pl.multiple_of(((yy * 2 + (1 - xlo if j else xlo)) * 2 + cc) * 256, 256)
         c = pltpu.make_async_copy(
-            nblk(yy, j, cc=cc), nw_out.at[:, pl.ds(off, 256)], w_s.at[len(puts)]
+            nblk(yy, j, cc=cc), nw_out.at[:, pl.ds(off, 256)], w_s
         )
         c.start()
-        puts.append(c)
 
     def await_(blk, i):
         cp(blk, blk, i, sib).wait_recv()
@@ -505,23 +472,25 @@
     await_(b, 8)
     for d in (0, 1):
         go(cp(b, b, 2 + d, to_y[d]))
+    for t in range(5, 8):
+        hgsend(t).start()
     go(cp(b, b, 10, sib))
     put(y, 1)
-    for t in range(5, 8):
-        hgsend(t, True).start()
     b = nblk(y2, 0)
     for d in (0, 1):
         await_(nblk(y2, 0, d), 4 + d)
-    go(cp(b, b, 6, to_x))
     go(cp(b, b, 15, sib))
     put(y2, 0)
     for d in (0, 1):
         b = nblk(from_y[d], 1)
         await_(b, 2 + d)
+        part = nblk(from_y[d], 1, d)
+        go(cp(part, part, 6 + d, to_y[d]))
         go(cp(b, b, 13 + d, sib))
         put(from_y[d], 1)
     b = nblk(y2, 1)
-    await_(b, 6)
+    for d in (0, 1):
+        await_(nblk(y2, 1, d), 6 + d)
     go(cp(b, b, 16, sib))
     put(y2, 1)
     oc = 1 - core
@@ -531,38 +500,23 @@
         await_(nblk(yy, j, cc=oc), 9 + i)
         put(yy, j, oc)
 
-    for t in range(8):
-        hgsend(t, False).wait_recv()
-    pltpu.make_async_copy(hts, hts, lsem.at[4]).wait()
-    for c in finals + puts:
+    got(hts, g_r)
+    got(hts, lsem.at[4])
+    for c in finals:
         c.wait()
-    for c in outs + sends:
-        c.wait_send()
-    for d in (0, 1):
-        hsend(d, True).wait_send()
-        for far in (0, 1):
-            wx(d, far, True).wait_send()
-            for j in range(4):
-                wy(j, d, far, True).wait_send()
-    for j in range(4):
-        wd(j).wait_send()
-    for t in range(8):
-        hgsend(t, True).wait_send()
-    for q in range(4):
-        for f in (0, 1):
-            gd(q, f).wait_send()
-            gyfar(q, f).wait_send()
-            gynear(q, f).wait_send()
-            if q >= 2 or f == 0:
-                xsend(q, f, True).wait_send()
-
-    def drain(k, c):
-        for hop in range(4):
-            for d in (0, 1):
-                zcopy(d, k, hop, True).wait_send()
-        return c
-
-    lax.fori_loop(0, NK, drain, 0)
+    got(nwb, w_s)
+    got(hts, g_s)
+    got(hts, hss)
+    got(cbuf.at[pl.ds(0, 7)], zs)
+    got(gs.at[0, 0, pl.ds(0, 336), :], wxs)
+    got(gs.at[pl.ds(0, 3), 0], wys)
+    got(gs.at[:, 0], wds)
+    got(gs, ds_)
+    got(yfs, yf_s)
+    got(yns, yn_s)
+    got(xs.at[pl.ds(0, 3)], x_s)
+    got(nr, n_s)
+    got(nwb.at[:, pl.ds(0, 3840)], o_s)
 
 
 def local(hidden, cotangent, master, moment_one, moment_two):
@@ -589,23 +543,23 @@
         v((FC, 256), F32),
         v((FC, 256), F32),
         v((FC, 4096), BF16),
-        v((3, 8, 128), F32),
-        v((3, 7, 8, 128), F32),
+        v((2, 8, 128), F32),
+        v((38, 8, 128), F32),
         dma((5,)),
         dma((NK,)),
-        dma((2, NK, 4)), dma((2, NK, 4)),
-        dma((2,)), dma((2,)),
-        dma((4,)), dma((4,)),
-        dma((4, 4)), dma((4, 4)),
-        dma((4,)), dma((4,)),
-        dma((4, 2)), dma((4, 2)),
-        dma((4, 2)), dma((4, 2)),
-        dma((4, 2)), dma((4, 2)),
-        dma((4, 2)), dma((2, 3)),
-        dma((8,)), dma((8,)),
-        dma((3, 7)), dma((3, 7)),
-        dma((17,)), dma((17,)),
-        dma((16,)),
+        dma, dma((NK, 4)),
+        dma, dma,
+        dma, dma((2,)),
+        dma, dma((2,)),
+        dma, dma,
+        dma, dma((4, 2)),
+        dma, dma((4, 2)),
+        dma, dma((4,)),
+        dma, dma,
+        dma, dma,
+        dma, dma((2,)),
+        dma, dma((17,)),
+        dma,
     ]
     sds = jax.ShapeDtypeStruct
     hg, nw, nm, n1, n2 = pl.pallas_call(

time: 156 us -> 152 us (0.974)
  Pallas kernels: 155 us -> 151 us
    pallas_call x1, Pallas kernels: 149 us -> 146 us  [local(): pl.pallas_call(kernel, out_shape=(sds((FC, 2048), BF16), sds((FC, 4096),...]
where the time goes in v3:
time: 152 us
  Pallas kernels  151 us (99%)
    pallas_call x1, Pallas kernels, local(): pl.pallas_call(kernel, out_shape=(sds((FC, 2048), BF16), sds((FC, 4096),...  146 us
    pallas_call x1, Pallas kernels, local(): pl.pallas_call(hand_on, out_shape=tuple((sds(t.shape, t.dtype) for t in o...  5.56 us

profile of v3, /device:TPU:1, one launch (start us, length us, event | category | flops | bytes accessed | tf_op | source)
XLA Modules:
  0.0 151.9 jit_solution(13582029586896239381)
XLA Ops:
  0.6 145.7 %fused_backward.1 = (bf16[448,2048]{1,0:T(8,128)(2,1)}, bf16[448,4096]{1,0:T(8,128)(2,1)}, f32[448,256]{1,0:T(8,128)}, f32[448,256]{1,0:T(8,128)}, f32[448,256]{1,0:T(8,128)}) custom-call(bf16[448,2048]{1,0:T(8,128)(2,1)} %bitcast.10, bf16[128,4096]{1,0:T(8,128)(2,1)} %cot.1, f32[448,256]{1,0:T(8,128)} %bitcast.12, f32[448,256]{1,0:T(8,128)} %bitcast.13, ...), custom_call_target="tpu_custom_call" | custom-call | flops 15032385536 | bytes 16000000 | tf_op jit(solution)/shard_map/fused_backward/pallas_call | solution.py:565
  146.3 5.6 %hand_on.1 = (bf16[448,2048]{1,0:T(8,128)(2,1)}, bf16[448,4096]{1,0:T(8,128)(2,1)}, f32[448,256]{1,0:T(8,128)}, f32[448,256]{1,0:T(8,128)}, f32[448,256]{1,0:T(8,128)}) custom-call(bf16[448,2048]{1,0:T(8,128)(2,1)} %get-tuple-element.15.refs_0_, bf16[448,4096]{1,0:T(8,128)(2,1)} %get-tuple-element.16.refs_1_, f32[448,256]{1,0:T(8,128)} %get-tuple-element.17.refs_2_, ...), custom_call_target="tpu_custom_call" | custom-call | tf_op jit(solution)/shard_map/hand_on/pallas_call | solution.py:586

commit v4 on v3

--- a/solution.py
+++ b/solution.py
@@ -118,14 +118,20 @@
         got(cbuf.at[k, pl.ds(0, 256 if hop < 3 else 128), :], zr.at[k, hop])
 
     def zring(s):
+        def forward(k, hop):
+            zwait(k, hop - 1)
+            for d in (0, 1):
+                zcopy(d, k, hop).start()
+
         for hop in (3, 2, 1):
-            k = s - hop
-
-            @pl.when((k >= 0) & (k < NK))
-            def _(hop=hop, k=k):
-                zwait(k, hop - 1)
-                for d in (0, 1):
-                    zcopy(d, k, hop).start()
+
+            @pl.when((s >= hop) & (s - hop < NK - 1))
+            def _(hop=hop):
+                forward(s - hop, hop)
+
+            @pl.when(s - hop == NK - 2)
+            def _(hop=hop):
+                forward(jnp.int32(NK - 1), hop)
 
         @pl.when(s < NK - 1)
         def _():
@@ -191,8 +197,9 @@
         @pl.when(part == 1)
         def _():
             for f in (0, 1):
+                own = jnp.dot(ht[f], cbuf[kc], preferred_element_type=F32)
                 gd(q, f).wait_recv()
-                gr[q, f] = gr[q, f] + jnp.dot(ht[f], cbuf[kc], preferred_element_type=F32)
+                gr[q, f] = gr[q, f] + own
                 yfs[q, f] = gr[q, f, :, lanes(y2)].astype(BF16)
                 gyfar(q, f).start()
             for f in (1, 0):
@@ -299,6 +306,10 @@
     pltpu.make_async_copy(hts, ht.at[h], lsem.at[4]).wait()
 
     def tick(s, c):
+        @pl.when(s >= 6)
+        def _():
+            gradient_chunk(s - 4)
+
         zring(s)
 
         @pl.when(s == 1)
@@ -338,13 +349,9 @@
         def _():
             gradient_chunk(jnp.int32(1))
 
-        @pl.when(s >= 6)
-        def _():
-            gradient_chunk(s - 4)
-
-        for q in range(3):
-
-            @pl.when(s == (7, 8, 10)[q])
+        for q in range(2):
+
+            @pl.when(s == (7, 8)[q])
             def _(q=q):
                 ystep2(q)
 
@@ -369,13 +376,15 @@
 
         return c
 
-    lax.fori_loop(1, 12, tick, 0)
-
+    lax.fori_loop(1, 11, tick, 0)
+
+    ystep2(2)
+    gradient_chunk(jnp.int32(7))
     hg_last(1 - h)
+    ystep3(2)
     for t in range(2):
         hgsend(t).start()
     ystep2(3)
-    ystep3(2)
     hg_last(h)
     own_hg_copy()
     ystep3(3)
@@ -396,15 +405,15 @@
     groups = [plane, [dev(zz=rem(z + i, 8)) for i in range(1, 8)]]
     base = 0
     for ph, group in enumerate(groups):
-        ns[ph] = sq
+        ns[ph] = jnp.sum(sq, axis=0, keepdims=True)
         for i, to in enumerate(group):
             rc(ns.at[ph], nr.at[base + i], n_s, n_r.at[ph], to).start()
         if ph == 1:
-            for t in range(2, 5):
+            for t in range(2, 4):
                 hgsend(t).start()
         heard = nr.at[pl.ds(base, len(group))]
         got(heard, n_r.at[ph])
-        sq = sq + jnp.sum(heard[...], axis=0)
+        sq = ns[ph] + jnp.sum(heard[...], axis=0)
         base += len(group)
     squares = jnp.sum(sq, keepdims=True)
     scale = jnp.minimum(1.0, 1.0 / (jnp.sqrt(squares) + 1e-06))
@@ -449,7 +458,8 @@
     def await_(blk, i):
         cp(blk, blk, i, sib).wait_recv()
 
-    go(cp(nblk(y, 0), nblk(y, 0), 8, to_x))
+    for i in (0, 1):
+        go(cp(nblk(y, 0, i), nblk(y, 0, i), 8 + 9 * i, to_x))
     for d in (0, 1):
         go(cp(nblk(y, 0), nblk(y, 0), d, to_y[d]))
     go(cp(nblk(y, 0), nblk(y, 0), 9, sib))
@@ -461,6 +471,9 @@
     ]
     for c in finals:
         c.start()
+    first, second = nblk(y, 1, 0), nblk(y, 1, 1)
+    await_(first, 8)
+    go(cp(first, first, 2, to_y[0]))
     for d in (0, 1):
         b = nblk(from_y[d], 0)
         await_(b, d)
@@ -468,12 +481,13 @@
         go(cp(part, part, 4 + d, to_y[d]))
         go(cp(b, b, 11 + d, sib))
         put(from_y[d], 0)
+    await_(second, 17)
+    go(cp(second, second, 3, to_y[1]))
+    go(cp(second, second, 18, to_y[0]))
+    go(cp(first, first, 19, to_y[1]))
+    for t in range(4, 8):
+        hgsend(t).start()
     b = nblk(y, 1)
-    await_(b, 8)
-    for d in (0, 1):
-        go(cp(b, b, 2 + d, to_y[d]))
-    for t in range(5, 8):
-        hgsend(t).start()
     go(cp(b, b, 10, sib))
     put(y, 1)
     b = nblk(y2, 0)
@@ -482,23 +496,33 @@
     go(cp(b, b, 15, sib))
     put(y2, 0)
     for d in (0, 1):
+        part = nblk(from_y[d], 1, d)
+        await_(part, 2 + d)
+        go(cp(part, part, 6 + d, to_y[d]))
+    for d in (0, 1):
+        await_(nblk(from_y[d], 1, 1 - d), 18 + d)
         b = nblk(from_y[d], 1)
-        await_(b, 2 + d)
-        part = nblk(from_y[d], 1, d)
-        go(cp(part, part, 6 + d, to_y[d]))
         go(cp(b, b, 13 + d, sib))
         put(from_y[d], 1)
+    oc = 1 - core
+
+    def from_sibling(yy, j, i):
+        await_(nblk(yy, j, cc=oc), i)
+        put(yy, j, oc)
+
+    from_sibling(y, 0, 9)
+    from_sibling(y, 1, 10)
+    from_sibling(yl1, 0, 11)
+    from_sibling(yr1, 0, 12)
+    from_sibling(y2, 0, 15)
     b = nblk(y2, 1)
     for d in (0, 1):
         await_(nblk(y2, 1, d), 6 + d)
     go(cp(b, b, 16, sib))
     put(y2, 1)
-    oc = 1 - core
-    for i, (yy, j) in enumerate(
-        ((y, 0), (y, 1), (yl1, 0), (yr1, 0), (yl1, 1), (yr1, 1), (y2, 0), (y2, 1))
-    ):
-        await_(nblk(yy, j, cc=oc), 9 + i)
-        put(yy, j, oc)
+    from_sibling(yl1, 1, 13)
+    from_sibling(yr1, 1, 14)
+    from_sibling(y2, 1, 16)
 
     got(hts, g_r)
     got(hts, lsem.at[4])
@@ -543,8 +567,8 @@
         v((FC, 256), F32),
         v((FC, 256), F32),
         v((FC, 4096), BF16),
-        v((2, 8, 128), F32),
-        v((38, 8, 128), F32),
+        v((2, 1, 128), F32),
+        v((38, 1, 128), F32),
         dma((5,)),
         dma((NK,)),
         dma, dma((NK, 4)),
@@ -558,7 +582,7 @@
         dma, dma,
         dma, dma,
         dma, dma((2,)),
-        dma, dma((17,)),
+        dma, dma((20,)),
         dma,
     ]
     sds = jax.ShapeDtypeStruct

time: 152 us -> 148 us (0.974)
  Pallas kernels: 151 us -> 148 us
    pallas_call x1, Pallas kernels: 146 us -> 142 us  [local(): pl.pallas_call(kernel, out_shape=(sds((FC, 2048), BF16), sds((FC, 4096),...]
where the time goes in v4:
time: 148 us
  Pallas kernels  148 us (100%)
    pallas_call x1, Pallas kernels, local(): pl.pallas_call(kernel, out_shape=(sds((FC, 2048), BF16), sds((FC, 4096),...  142 us
    pallas_call x1, Pallas kernels, local(): pl.pallas_call(hand_on, out_shape=tuple((sds(t.shape, t.dtype) for t in o...  5.56 us

profile of v4, /device:TPU:1, one launch (start us, length us, event | category | flops | bytes accessed | tf_op | source)
XLA Modules:
  0.0 148.3 jit_solution(1316579882220705662)
XLA Ops:
  0.6 142.1 %fused_backward.1 = (bf16[448,2048]{1,0:T(8,128)(2,1)}, bf16[448,4096]{1,0:T(8,128)(2,1)}, f32[448,256]{1,0:T(8,128)}, f32[448,256]{1,0:T(8,128)}, f32[448,256]{1,0:T(8,128)}) custom-call(bf16[448,2048]{1,0:T(8,128)(2,1)} %bitcast.10, bf16[128,4096]{1,0:T(8,128)(2,1)} %cot.1, f32[448,256]{1,0:T(8,128)} %bitcast.12, f32[448,256]{1,0:T(8,128)} %bitcast.13, ...), custom_call_target="tpu_custom_call" | custom-call | flops 15032385536 | bytes 16000000 | tf_op jit(solution)/shard_map/fused_backward/pallas_call | solution.py:589
  142.7 5.6 %hand_on.1 = (bf16[448,2048]{1,0:T(8,128)(2,1)}, bf16[448,4096]{1,0:T(8,128)(2,1)}, f32[448,256]{1,0:T(8,128)}, f32[448,256]{1,0:T(8,128)}, f32[448,256]{1,0:T(8,128)}) custom-call(bf16[448,2048]{1,0:T(8,128)(2,1)} %get-tuple-element.15.refs_0_, bf16[448,4096]{1,0:T(8,128)(2,1)} %get-tuple-element.16.refs_1_, f32[448,256]{1,0:T(8,128)} %get-tuple-element.17.refs_2_, ...), custom_call_target="tpu_custom_call" | custom-call | tf_op jit(solution)/shard_map/hand_on/pallas_call | solution.py:610

commit v5 on v4

--- a/solution.py
+++ b/solution.py
@@ -84,11 +84,8 @@
 
     barrier = pltpu.get_barrier_semaphore()
     peers = [sib]
-    plane = [
-        dev(xx=rem(x + i, 4), yy=rem(y + j, 4), cc=1 - core if c else core)
-        for j in range(4) for i in range(4) for c in (0, 1) if i + j + c
-    ]
-    peers = list(plane)
+    peers = [dev(xx=rem(x + i, 4), cc=1 - core if c else core) for i in range(4) for c in (0, 1) if i + c]
+    peers += [dev(yy=rem(y + i, 4)) for i in range(1, 4)]
     peers += [dev(zz=rem(z + i, 8)) for i in range(1, 8)]
     for to in peers:
         pl.semaphore_signal(barrier, inc=1, device_id=to, device_id_type=MESH)
@@ -402,13 +399,17 @@
         ga[half] = g
         sq = sq + jnp.sum((g * g).reshape(FC // 8, 8, 128), axis=0)
 
-    groups = [plane, [dev(zz=rem(z + i, 8)) for i in range(1, 8)]]
+    groups = [
+        [dev(xx=rem(x + i, 4), cc=1 - core if c else core) for i in range(4) for c in (0, 1) if i + c],
+        [dev(yy=rem(y + i, 4)) for i in range(1, 4)],
+        [dev(zz=rem(z + i, 8)) for i in range(1, 8)],
+    ]
     base = 0
     for ph, group in enumerate(groups):
         ns[ph] = jnp.sum(sq, axis=0, keepdims=True)
         for i, to in enumerate(group):
             rc(ns.at[ph], nr.at[base + i], n_s, n_r.at[ph], to).start()
-        if ph == 1:
+        if ph == 2:
             for t in range(2, 4):
                 hgsend(t).start()
         heard = nr.at[pl.ds(base, len(group))]
@@ -567,8 +568,8 @@
         v((FC, 256), F32),
         v((FC, 256), F32),
         v((FC, 4096), BF16),
-        v((2, 1, 128), F32),
-        v((38, 1, 128), F32),
+        v((3, 1, 128), F32),
+        v((17, 1, 128), F32),
         dma((5,)),
         dma((NK,)),
         dma, dma((NK, 4)),
@@ -581,7 +582,7 @@
         dma, dma((4,)),
         dma, dma,
         dma, dma,
-        dma, dma((2,)),
+        dma, dma((3,)),
         dma, dma((20,)),
         dma,
     ]

time: 148 us -> 147 us (level)
  no operation moved by 1% of the time
where the time goes in v5:
time: 147 us
  Pallas kernels  147 us (100%)
    pallas_call x1, Pallas kernels, local(): pl.pallas_call(kernel, out_shape=(sds((FC, 2048), BF16), sds((FC, 4096),...  141 us
    pallas_call x1, Pallas kernels, local(): pl.pallas_call(hand_on, out_shape=tuple((sds(t.shape, t.dtype) for t in o...  5.56 us

profile of v5, /device:TPU:1, one launch (start us, length us, event | category | flops | bytes accessed | tf_op | source)
XLA Modules:
  0.0 147.2 jit_solution(2482137130217177201)
XLA Ops:
  0.6 141.0 %fused_backward.1 = (bf16[448,2048]{1,0:T(8,128)(2,1)}, bf16[448,4096]{1,0:T(8,128)(2,1)}, f32[448,256]{1,0:T(8,128)}, f32[448,256]{1,0:T(8,128)}, f32[448,256]{1,0:T(8,128)}) custom-call(bf16[448,2048]{1,0:T(8,128)(2,1)} %bitcast.10, bf16[128,4096]{1,0:T(8,128)(2,1)} %cot.1, f32[448,256]{1,0:T(8,128)} %bitcast.12, f32[448,256]{1,0:T(8,128)} %bitcast.13, ...), custom_call_target="tpu_custom_call" | custom-call | flops 15032385536 | bytes 16000000 | tf_op jit(solution)/shard_map/fused_backward/pallas_call | solution.py:590
  141.6 5.6 %hand_on.1 = (bf16[448,2048]{1,0:T(8,128)(2,1)}, bf16[448,4096]{1,0:T(8,128)(2,1)}, f32[448,256]{1,0:T(8,128)}, f32[448,256]{1,0:T(8,128)}, f32[448,256]{1,0:T(8,128)}) custom-call(bf16[448,2048]{1,0:T(8,128)(2,1)} %get-tuple-element.15.refs_0_, bf16[448,4096]{1,0:T(8,128)(2,1)} %get-tuple-element.16.refs_1_, f32[448,256]{1,0:T(8,128)} %get-tuple-element.17.refs_2_, ...), custom_call_target="tpu_custom_call" | custom-call | tf_op jit(solution)/shard_map/hand_on/pallas_call | solution.py:611

commit v6 on v5

--- a/solution.py
+++ b/solution.py
@@ -461,8 +461,10 @@
 
     for i in (0, 1):
         go(cp(nblk(y, 0, i), nblk(y, 0, i), 8 + 9 * i, to_x))
-    for d in (0, 1):
-        go(cp(nblk(y, 0), nblk(y, 0), d, to_y[d]))
+    for i in (0, 1):
+        for d in (0, 1):
+            part = nblk(y, 0, d if i == 0 else 1 - d)
+            go(cp(part, part, d + 20 * i, to_y[d]))
     go(cp(nblk(y, 0), nblk(y, 0), 9, sib))
     put(y, 0)
     finals = [
@@ -476,10 +478,12 @@
     await_(first, 8)
     go(cp(first, first, 2, to_y[0]))
     for d in (0, 1):
+        part = nblk(from_y[d], 0, d)
+        await_(part, d)
+        go(cp(part, part, 4 + d, to_y[d]))
+    for d in (0, 1):
+        await_(nblk(from_y[d], 0, 1 - d), 20 + d)
         b = nblk(from_y[d], 0)
-        await_(b, d)
-        part = nblk(from_y[d], 0, d)
-        go(cp(part, part, 4 + d, to_y[d]))
         go(cp(b, b, 11 + d, sib))
         put(from_y[d], 0)
     await_(second, 17)
@@ -583,7 +587,7 @@
         dma, dma,
         dma, dma,
         dma, dma((3,)),
-        dma, dma((20,)),
+        dma, dma((22,)),
         dma,
     ]
     sds = jax.ShapeDtypeStruct

time: 147 us -> 147 us (level)
  no operation moved by 1% of the time
where the time goes in v6:
time: 147 us
  Pallas kernels  146 us (99%)
    pallas_call x1, Pallas kernels, local(): pl.pallas_call(kernel, out_shape=(sds((FC, 2048), BF16), sds((FC, 4096),...  141 us
    pallas_call x1, Pallas kernels, local(): pl.pallas_call(hand_on, out_shape=tuple((sds(t.shape, t.dtype) for t in o...  5.56 us

profile of v6, /device:TPU:1, one launch (start us, length us, event | category | flops | bytes accessed | tf_op | source)
XLA Modules:
  0.0 147.0 jit_solution(804837495262994465)
XLA Ops:
  0.6 140.8 %fused_backward.1 = (bf16[448,2048]{1,0:T(8,128)(2,1)}, bf16[448,4096]{1,0:T(8,128)(2,1)}, f32[448,256]{1,0:T(8,128)}, f32[448,256]{1,0:T(8,128)}, f32[448,256]{1,0:T(8,128)}) custom-call(bf16[448,2048]{1,0:T(8,128)(2,1)} %bitcast.10, bf16[128,4096]{1,0:T(8,128)(2,1)} %cot.1, f32[448,256]{1,0:T(8,128)} %bitcast.12, f32[448,256]{1,0:T(8,128)} %bitcast.13, ...), custom_call_target="tpu_custom_call" | custom-call | flops 15032385536 | bytes 16000000 | tf_op jit(solution)/shard_map/fused_backward/pallas_call | solution.py:594
  141.4 5.6 %hand_on.1 = (bf16[448,2048]{1,0:T(8,128)(2,1)}, bf16[448,4096]{1,0:T(8,128)(2,1)}, f32[448,256]{1,0:T(8,128)}, f32[448,256]{1,0:T(8,128)}, f32[448,256]{1,0:T(8,128)}) custom-call(bf16[448,2048]{1,0:T(8,128)(2,1)} %get-tuple-element.15.refs_0_, bf16[448,4096]{1,0:T(8,128)(2,1)} %get-tuple-element.16.refs_1_, f32[448,256]{1,0:T(8,128)} %get-tuple-element.17.refs_2_, ...), custom_call_target="tpu_custom_call" | custom-call | tf_op jit(solution)/shard_map/hand_on/pallas_call | solution.py:615
